TPU v7x, 256 devices: a whole 4x4x8 slice. The times are simulated.
256 devices in a mesh: elem: 32 (over y, z), col: 8 (over x, core).
Axes of the slice: x: 4, y: 4, z: 8, core: 2. Of those that a mesh axis runs over, the one named last changes fastest.
Arguments:
- state: float32 [7, 72, 16, 32768], P(None, None, None, ('elem', 'col')), may hold values from -6 to 6
- metric: float32 [2, 16, 32768], P(None, None, ('elem', 'col')), may hold values from 0.5 to 2
- edge_peer: int32 [4, 32768], P(None, ('elem', 'col')), may hold values from 0 to 32767, as said below
- edge_code: int32 [4, 32768], P(None, ('elem', 'col')), may hold values from 0 to 7, as said below
- span_owner: int32 [4096, 1], P(('elem', 'col')), may hold values from 0 to 7; in each aligned block of 16 rows (0 to 15, 16 to 31, ...) at most 3 rows name the same one
- work_class: int32 [16, 32768], P(None, ('elem', 'col')), may hold values from 0 to 3
Outputs:
- new_state: float32 [7, 72, 16, 32768], P(None, None, None, ('elem', 'col'))
- rain_by_owner: float32 [32, 8, 24, 128], P('elem', 'col')
Inputs may be any that keep to these rules, and one draw needn't show every extreme that they name: `edge_peer`: elements are numbered device by device along elem+col, 128 to a device. Every edge neighbour lies on the element's own device or on the device directly before or after it along elem+col, which closes into a loop; at most 64 edges of a device's elements meet the next device, and at most as many the previous one. The relation is symmetric: if edge k of element a meets edge k2 of element b, then edge k2 of b meets edge k of a with the same reversal. `edge_code`: the code is 2 k2 + r, where k2 is the neighbour's edge and r is 1 if the two edges number their points in opposite orders. `span_owner`: among the 16 spans of one device no owner is named more than 3 times, and in some device one owner is named exactly 3 times.
All inputs are finite; a program needn't handle non-finite values.
Results may differ from a plain program's by a relative error of at most 0.0003.
Values sent between devices are 32-bit elements; how exact they have to be, the bound alone decides.
No kernel may reach another device: no remote copies, remote signals or barrier semaphores. Data moves between devices by JAX's collectives and lax.ppermute only.
A program may use at most 128 MiB of HBM per device.

v0:
```python
import jax
import jax.numpy as jnp
import numpy as np
from jax import lax
from jax.experimental import pallas as pl
from jax.experimental.pallas import tpu as pltpu
from jax.sharding import PartitionSpec as P

LEV = 72
GROUPS = LEV // 8
ROWS = LEV * 16
LANES = 128
EDGE_POINTS = ((0, 1, 2, 3), (3, 7, 11, 15), (12, 13, 14, 15), (0, 4, 8, 12))
RIM_POINTS = (0, 1, 2, 3, 4, 7, 8, 11, 12, 13, 14, 15)
CORNERS = (0, 3, 12, 15)
SCALE = 0.5 * 0.03
FIRST = (2, 3, 4)
SECOND = (0, 1, 5, 6)
CAP = 3
F32 = jnp.float32
BF16 = jnp.bfloat16
VMEM_LIMIT = 40 * 1024 * 1024


def derivative_matrix():
    nodes = np.array([-1.0, -1.0 / np.sqrt(5.0), 1.0 / np.sqrt(5.0), 1.0])
    weights = np.array(
        [1.0 / np.prod([nodes[a] - nodes[b] for b in range(4) if b != a]) for a in range(4)]
    )
    table = np.zeros((4, 4))
    for a in range(4):
        for b in range(4):
            if a != b:
                table[a, b] = weights[b] / weights[a] / (nodes[a] - nodes[b])
        table[a, a] = -table[a].sum()
    return table


DG = derivative_matrix()
EVEN0 = float((DG[0, 0] + DG[0, 3]) / 2)
EVEN1 = float((DG[1, 0] + DG[1, 3]) / 2)
ODD00 = float((DG[0, 0] - DG[0, 3]) / 2)
ODD01 = float((DG[0, 1] - DG[0, 2]) / 2)
ODD10 = float((DG[1, 0] - DG[1, 3]) / 2)
ODD11 = float((DG[1, 1] - DG[1, 2]) / 2)


def derive(u0, u1, u2, u3):
    even = (u0 + u3) - (u1 + u2)
    o0 = u0 - u3
    o1 = u1 - u2
    a0 = EVEN0 * even
    a1 = EVEN1 * even
    b0 = ODD00 * o0 + ODD01 * o1
    b1 = ODD10 * o0 + ODD11 * o1
    return a0 + b0, a1 + b1, b1 - a1, b0 - a0


def scaled_tendency(u, metric):
    total = [None] * 16
    for b in range(4):
        points = [4 * b + a for a in range(4)]
        flux = derive(*[u[p] for p in points])
        for p, value in zip(points, derive(*[f * metric(0, p) for f, p in zip(flux, points)])):
            total[p] = value
    for a in range(4):
        points = [a + 4 * b for b in range(4)]
        flux = derive(*[u[p] for p in points])
        for p, value in zip(points, derive(*[f * metric(1, p) for f, p in zip(flux, points)])):
            total[p] = total[p] + value
    return total


def edge_rows(peer_ref, code_ref, me, devices):
    rows = []
    for k in range(4):
        peer = peer_ref[k : k + 1, :]
        code = code_ref[k : k + 1, :]
        offset = lax.shift_right_logical(peer, 7) - me
        source = lax.shift_right_logical(code, 1) * LANES + lax.bitwise_and(peer, LANES - 1)
        rows.append(
            dict(
                source=source,
                own=offset == 0,
                after=(offset == 1) | (offset == 1 - devices),
                before=(offset == -1) | (offset == devices - 1),
            )
        )
    return rows


def one_hot(mask):
    return jnp.where(mask, 1.0, 0.0).astype(BF16)


def pack_weights(rows, hit_ref, less_ref, pack_ref):
    number = lax.broadcasted_iota(jnp.int32, (512, LANES), 0)
    for k, row in enumerate(rows):
        hit_ref[:, k * LANES : (k + 1) * LANES] = one_hot((number == row["source"]) & row["before"])
        less_ref[:, k * LANES : (k + 1) * LANES] = one_hot(number < row["source"])
    met = lax.dot_general(
        jnp.ones((16, 512), BF16), hit_ref[...], (((1,), (1,)), ((), ())), preferred_element_type=F32
    )
    before_slot = jnp.dot(met.astype(BF16), less_ref[...], preferred_element_type=F32)
    lane = lax.broadcasted_iota(jnp.int32, (512, LANES), 1)
    for k in range(4):
        less_ref[:, k * LANES : (k + 1) * LANES] = one_hot(number < lane + k * LANES)
    meets = jnp.concatenate([jnp.where(row["after"], 1.0, 0.0) for row in rows], axis=1)
    after_slot = jnp.dot(
        jnp.broadcast_to(meets, (16, 512)).astype(BF16), less_ref[...], preferred_element_type=F32
    )
    slot = lax.broadcasted_iota(jnp.int32, (64, LANES), 0)
    zero = jnp.zeros((64, LANES), BF16)
    for k, row in enumerate(rows):
        low = slice(k * LANES, (k + 1) * LANES)
        high = slice(512 + k * LANES, 512 + (k + 1) * LANES)
        after = one_hot((slot == after_slot[0:1, low].astype(jnp.int32)) & row["after"])
        before = one_hot((slot == before_slot[0:1, low].astype(jnp.int32)) & row["before"])
        pack_ref[0:64, low] = after
        pack_ref[0:64, high] = zero
        pack_ref[64:128, low] = zero
        pack_ref[64:128, high] = after
        pack_ref[128:192, low] = before
        pack_ref[128:192, high] = zero
        pack_ref[192:256, low] = zero
        pack_ref[192:256, high] = before


def edges_out(count, state_ref, metric_ref, pack_ref, acc_ref, high_ref, low_ref, after_ref, before_ref):
    def metric(direction, point):
        return jnp.broadcast_to(
            SCALE * metric_ref[16 * direction + point : 16 * direction + point + 1, :], (8, LANES)
        )

    def group(index, carry):
        base = index * 128
        u = [state_ref[pl.ds(base + p, 8, stride=16), :] for p in range(16)]
        tendency = scaled_tendency(u, metric)
        for p in range(16):
            if p in CORNERS:
                value = u[p]
            elif p in RIM_POINTS:
                value = u[p] + tendency[p]
            else:
                value = u[p] + 2.0 * tendency[p]
            acc_ref[pl.ds(pl.multiple_of(base + 8 * p, 8), 8), :] = value
        top = {p: tendency[p].astype(BF16).astype(F32) for p in RIM_POINTS}
        rest = {p: tendency[p] - top[p] for p in RIM_POINTS}
        rows = pl.ds(pl.multiple_of(index * 16, 16), 16)
        for k in range(4):
            for half in range(2):
                first, second = EDGE_POINTS[k][2 * half : 2 * half + 2]
                place = slice(half * 512 + k * LANES, half * 512 + (k + 1) * LANES)
                high_ref[rows, place] = jnp.concatenate([top[first], top[second]], 0).astype(BF16)
                low_ref[rows, place] = jnp.concatenate([rest[first], rest[second]], 0).astype(BF16)
        return carry

    lax.fori_loop(0, count * GROUPS, group, 0)
    across = (((1,), (1,)), ((), ()))
    packed = lax.dot_general(
        high_ref[...], pack_ref[...], across, preferred_element_type=F32
    ) + lax.dot_general(low_ref[...], pack_ref[...], across, preferred_element_type=F32)
    after_ref[...] = packed[:, :LANES]
    before_ref[...] = packed[:, LANES:]


def first_kernel(devices, state_ref, metric_ref, peer_ref, code_ref,
                 acc_ref, high_ref, low_ref, pack_ref, after_ref, before_ref,
                 held_ref, hit_ref, less_ref, sem):
    me = lax.axis_index(("elem", "col"))
    copy = pltpu.make_async_copy(
        state_ref.at[pl.ds(FIRST[0] * ROWS, len(FIRST) * ROWS)], held_ref, sem
    )
    copy.start()
    pack_weights(edge_rows(peer_ref, code_ref, me, devices), hit_ref, less_ref, pack_ref)
    copy.wait()
    edges_out(len(FIRST), held_ref, metric_ref, pack_ref, acc_ref, high_ref, low_ref, after_ref, before_ref)


def second_kernel(devices, state_ref, metric_ref, peer_ref, code_ref, pack_ref,
                  acc_ref, high_ref, low_ref, own_ref, after_ref, before_ref,
                  held_ref, sems):
    me = lax.axis_index(("elem", "col"))
    copies = [
        pltpu.make_async_copy(
            state_ref.at[pl.ds(0, 2 * ROWS)], held_ref.at[pl.ds(0, 2 * ROWS)], sems.at[0]
        ),
        pltpu.make_async_copy(
            state_ref.at[pl.ds(5 * ROWS, 2 * ROWS)], held_ref.at[pl.ds(2 * ROWS, 2 * ROWS)], sems.at[1]
        ),
    ]
    for copy in copies:
        copy.start()
    number = lax.broadcasted_iota(jnp.int32, (512, LANES), 0)
    for k, row in enumerate(edge_rows(peer_ref, code_ref, me, devices)):
        own_ref[:, k * LANES : (k + 1) * LANES] = one_hot((number == row["source"]) & row["own"])
    for copy in copies:
        copy.wait()
    edges_out(len(SECOND), held_ref, metric_ref, pack_ref, acc_ref, high_ref, low_ref, after_ref, before_ref)


def split(value):
    top = value.astype(BF16)
    return top, (value - top.astype(F32)).astype(BF16)


def averaged(count, code_ref, acc_ref, high_ref, low_ref, own_ref, pack_ref, from_before_ref,
             from_after_ref, lines_ref, dyn_ref):
    top_next, rest_next = split(from_after_ref[...])
    top_last, rest_last = split(from_before_ref[...])
    top = jnp.concatenate([top_next, top_last], axis=1)
    rest = jnp.concatenate([rest_next, rest_last], axis=1)
    for half in range(2):
        place = slice(half * 512, (half + 1) * 512)
        lines_ref[:, place] = (
            jnp.dot(high_ref[:, place], own_ref[...], preferred_element_type=F32)
            + jnp.dot(low_ref[:, place], own_ref[...], preferred_element_type=F32)
            + jnp.dot(top, pack_ref[:, place], preferred_element_type=F32)
            + jnp.dot(rest, pack_ref[:, place], preferred_element_type=F32)
        )
    turned = [
        jnp.broadcast_to(lax.bitwise_and(code_ref[k : k + 1, :], 1), (8, LANES)) == 1 for k in range(4)
    ]

    def group(index, carry):
        base = index * 128
        value = [acc_ref[pl.ds(pl.multiple_of(base + 8 * p, 8), 8), :] for p in range(16)]
        for k in range(4):
            line = []
            for half in range(2):
                place = slice(half * 512 + k * LANES, half * 512 + (k + 1) * LANES)
                for second in range(2):
                    rows = pl.ds(pl.multiple_of(index * 16 + 8 * second, 8), 8)
                    line.append(lines_ref[rows, place])
            for t in range(4):
                p = EDGE_POINTS[k][t]
                value[p] = value[p] + jnp.where(turned[k], line[3 - t], line[t])
        for p in range(16):
            dyn_ref[pl.ds(base + p, 8, stride=16), :] = value[p]
        return carry

    lax.fori_loop(0, count * GROUPS, group, 0)


def softplus(x):
    tail = jnp.exp(-jnp.abs(x))
    small = tail - 0.5 * tail * tail
    return jnp.maximum(x, 0.0) + jnp.where(tail < 1e-3, small, jnp.log(1.0 + tail))


UNROLL = 8


def physics(dyn_ref, mark_ref):
    work = mark_ref[...]
    marks = [jnp.where(work >= section, 0.3, 0.0) for section in (1, 2, 3)]

    def condense(block, rain):
        base = pl.multiple_of(block * (16 * UNROLL), 16)
        for step in range(UNROLL):
            heat_at = pl.ds(base + 16 * step, 16)
            vapour_at = pl.ds(ROWS + base + 16 * step, 16)
            water_at = pl.ds(2 * ROWS + base + 16 * step, 16)
            heat = dyn_ref[heat_at, :]
            vapour = dyn_ref[vapour_at, :]
            excess = vapour - 0.5 * heat
            total = None
            for mark in marks:
                amount = mark * softplus(excess)
                excess = excess - 1.25 * amount
                total = amount if total is None else total + amount
            dyn_ref[heat_at, :] = heat + 0.5 * total
            dyn_ref[vapour_at, :] = vapour - total
            dyn_ref[water_at, :] = dyn_ref[water_at, :] + total
            rain = rain + total
        return rain

    return lax.fori_loop(0, LEV // UNROLL, condense, jnp.zeros((16, LANES), F32))


def mixed(dyn_ref, out_ref):
    for var in range(3):
        start = var * ROWS

        def at(level, start=start):
            return dyn_ref[pl.ds(start + 16 * level, 16), :]

        upper = here = at(0)
        for level in range(LEV):
            lower = at(min(level + 1, LEV - 1))
            out_ref[pl.ds(start + 16 * level, 16), :] = 0.5 * here + 0.25 * (upper + lower)
            upper, here = here, lower


def by_span(rain):
    point = lax.broadcasted_iota(jnp.int32, (16, LANES), 0)
    eighth = lax.shift_right_logical(lax.broadcasted_iota(jnp.int32, (16, LANES), 1), 3)
    total = None
    for shift in range(16):
        moved = pltpu.roll(rain, 8 * shift, 1) if shift else rain
        kept = jnp.where(point == eighth, moved, 0.0)
        kept = pltpu.roll(kept, 16 - shift, 0) if shift else kept
        total = kept if total is None else total + kept
    return total


def third_kernel(owner_ref, code_ref, mark_ref, acc_ref, high_ref, low_ref, own_ref, pack_ref,
                 from_before_ref, from_after_ref, state_out, rain_ref,
                 lines_ref, dyn_ref, mixed_ref, rain_rows, counts, sem):
    averaged(len(FIRST), code_ref, acc_ref, high_ref, low_ref, own_ref, pack_ref, from_before_ref,
             from_after_ref, lines_ref, dyn_ref)
    rain = physics(dyn_ref, mark_ref)
    mixed(dyn_ref, mixed_ref)
    copy = pltpu.make_async_copy(
        mixed_ref, state_out.at[pl.ds(FIRST[0] * ROWS, len(FIRST) * ROWS)], sem
    )
    copy.start()
    rain_rows[...] = by_span(rain) * (1.0 / LEV)
    rain_ref[...] = jnp.zeros_like(rain_ref)
    for owner in range(8):
        counts[owner] = 0
    for span in range(16):
        owner = owner_ref[span]
        rank = counts[owner]
        counts[owner] = rank + 1
        rain_ref[pl.ds(owner * CAP + rank, 1), :] = rain_rows[span : span + 1, :]
    copy.wait()


def fourth_kernel(code_ref, acc_ref, high_ref, low_ref, own_ref, pack_ref, from_before_ref,
                  from_after_ref, state_in, state_out, lines_ref, dyn_ref, sems):
    del state_in
    averaged(len(SECOND), code_ref, acc_ref, high_ref, low_ref, own_ref, pack_ref, from_before_ref,
             from_after_ref, lines_ref, dyn_ref)
    copies = [
        pltpu.make_async_copy(
            dyn_ref.at[pl.ds(0, 2 * ROWS)], state_out.at[pl.ds(0, 2 * ROWS)], sems.at[0]
        ),
        pltpu.make_async_copy(
            dyn_ref.at[pl.ds(2 * ROWS, 2 * ROWS)], state_out.at[pl.ds(5 * ROWS, 2 * ROWS)], sems.at[1]
        ),
    ]
    for copy in copies:
        copy.start()
    for copy in copies:
        copy.wait()


def passed_along(value, axis, steps):
    count = lax.axis_size(axis)
    pairs = [(source, (source + steps) % count) for source in range(count)]
    return lax.ppermute(value, axis, pairs)


VM = pl.BlockSpec(memory_space=pltpu.VMEM)
SM = pl.BlockSpec(memory_space=pltpu.SMEM)
ANY = pl.BlockSpec(memory_space=pl.ANY)


def shape(*sizes, dtype=F32):
    return jax.ShapeDtypeStruct(sizes, dtype)


def call(kernel, out, ins, outs, scratch, cost, **more):
    return pl.pallas_call(
        kernel,
        out_shape=out,
        in_specs=ins,
        out_specs=outs,
        scratch_shapes=scratch,
        cost_estimate=pl.CostEstimate(flops=cost, bytes_accessed=4 << 20, transcendentals=0),
        compiler_params=pltpu.CompilerParams(vmem_limit_bytes=VMEM_LIMIT),
        **more,
    )


def body(state, metric, edge_peer, edge_code, span_owner, work_class):
    axes = ("elem", "col")
    devices = lax.axis_size(axes)
    state = state.reshape(7 * ROWS, LANES)
    metric = metric.reshape(32, LANES)
    owner = span_owner.reshape(16)
    n1, n2 = len(FIRST), len(SECOND)

    def sizes(count):
        return [
            shape(count * ROWS, LANES),
            shape(count * 144, 1024, dtype=BF16),
            shape(count * 144, 1024, dtype=BF16),
        ]

    acc1, high1, low1, pack, after1, before1 = call(
        lambda *refs: first_kernel(devices, *refs),
        sizes(n1) + [shape(256, 1024, dtype=BF16), shape(n1 * 144, LANES), shape(n1 * 144, LANES)],
        [ANY, VM, VM, VM],
        [VM] * 6,
        [
            pltpu.VMEM((n1 * ROWS, LANES), F32),
            pltpu.VMEM((512, 512), BF16),
            pltpu.VMEM((512, 512), BF16),
            pltpu.SemaphoreType.DMA,
        ],
        500_000_000,
    )(state, metric, edge_peer, edge_code)
    from_before1 = passed_along(after1, axes, 1)
    from_after1 = passed_along(before1, axes, -1)
    acc2, high2, low2, own, after2, before2 = call(
        lambda *refs: second_kernel(devices, *refs),
        sizes(n2) + [shape(512, 512, dtype=BF16), shape(n2 * 144, LANES), shape(n2 * 144, LANES)],
        [ANY, VM, VM, VM, VM],
        [VM] * 6,
        [pltpu.VMEM((n2 * ROWS, LANES), F32), pltpu.SemaphoreType.DMA((2,))],
        500_000_000,
    )(state, metric, edge_peer, edge_code, pack)
    from_before2 = passed_along(after2, axes, 1)
    from_after2 = passed_along(before2, axes, -1)
    new_state, rain = call(
        third_kernel,
        [shape(7 * ROWS, LANES), shape(8 * CAP, LANES)],
        [SM] + [VM] * 9,
        [ANY, VM],
        [
            pltpu.VMEM((n1 * 144, 1024), F32),
            pltpu.VMEM((n1 * ROWS, LANES), F32),
            pltpu.VMEM((n1 * ROWS, LANES), F32),
            pltpu.VMEM((16, LANES), F32),
            pltpu.SMEM((8,), jnp.int32),
            pltpu.SemaphoreType.DMA,
        ],
        2_000_000_000,
    )(
        owner, edge_code, work_class, acc1, high1, low1, own, pack, from_before1, from_after1
    )
    rain = lax.all_to_all(rain.reshape(8, CAP, LANES), "col", split_axis=0, concat_axis=0, tiled=True)
    new_state = call(
        fourth_kernel,
        shape(7 * ROWS, LANES),
        [VM] * 8 + [ANY],
        ANY,
        [
            pltpu.VMEM((n2 * 144, 1024), F32),
            pltpu.VMEM((n2 * ROWS, LANES), F32),
            pltpu.SemaphoreType.DMA((2,)),
        ],
        2_000_000_000,
        input_output_aliases={8: 0},
    )(edge_code, acc2, high2, low2, own, pack, from_before2, from_after2, new_state)
    return new_state.reshape(7, LEV, 16, LANES), rain.reshape(1, 1, 8 * CAP, LANES)


def solution(mesh):
    placed = (
        P(None, None, None, ("elem", "col")),
        P(None, None, ("elem", "col")),
        P(None, ("elem", "col")),
        P(None, ("elem", "col")),
        P(("elem", "col"), None),
        P(None, ("elem", "col")),
    )
    return jax.shard_map(
        body,
        mesh=mesh,
        in_specs=placed,
        out_specs=(P(None, None, None, ("elem", "col")), P("elem", "col", None, None)),
        check_vma=False,
    )
```

profile of v0, /device:TPU:1, one launch (start us, length us, event | category | flops | bytes accessed | tf_op | source)
XLA Modules:
  0.0 54.8 jit_solution(1916553431161456995)
XLA Ops:
  0.6 2.2 %copy-done = f32[7,72,16,128]{3,2,1,0:T(8,128)S(1)} copy-done((f32[7,72,16,128]{3,2,1,0:T(8,128)S(1)}, f32[7,72,16,128]{3,2,1,0:T(8,128)}, u32[]{:S(2)}) %copy-start) | copy-done | bytes 4128792
  2.8 0.7 %copy-done.5 = f32[2,16,128]{2,1,0:T(8,128)S(1)} copy-done((f32[2,16,128]{2,1,0:T(8,128)S(1)}, f32[2,16,128]{2,1,0:T(8,128)}, u32[]{:S(2)}) %copy-start.5) | copy-done | bytes 16408
  3.5 0.7 %copy-done.6 = s32[4,128]{1,0:T(4,128)S(1)} copy-done((s32[4,128]{1,0:T(4,128)S(1)}, s32[4,128]{1,0:T(4,128)}, u32[]{:S(2)}) %copy-start.6) | copy-done | bytes 2072
  4.2 0.7 %copy-done.8 = s32[4,128]{1,0:T(4,128)S(1)} copy-done((s32[4,128]{1,0:T(4,128)S(1)}, s32[4,128]{1,0:T(4,128)}, u32[]{:S(2)}) %copy-start.8) | copy-done | bytes 2072
  4.9 3.7 %shard_map.77 = (f32[3456,128]{1,0:T(8,128)S(1)}, bf16[432,1024]{1,0:T(8,128)(2,1)S(1)}, bf16[432,1024]{1,0:T(8,128)(2,1)S(1)}, bf16[256,1024]{1,0:T(8,128)(2,1)...) custom-call(f32[8064,128]{1,0:T(8,128)S(1)} %bitcast.4, f32[32,128]{1,0:T(8,128)S(1)} %bitcast.6, ...), custom_call_target="tpu_custom_call" | custom-call | flops 500000000 | bytes 4194304 | tf_op jit(solution)/shard_map/pallas_call | solution.py:392
  8.6 0.0 copy-start.9
  8.6 0.0 copy-start.10
  8.7 2.7 %collective-permute-start.2 = (f32[432,128]{1,0:T(8,128)S(1)}, f32[432,128]{1,0:T(8,128)S(1)}, u32[]{:S(2)}, u32[]{:S(2)}) collective-permute-start(f32[432,128]{1,0:T(8,128)S(1)} %get-tuple-element.26), channel_id=1, source_target_pairs={{0,1},{1,2},{2,3},{3,4},{4,5},{5,6},{6,7},{7,8},{8,9},{9,10},{10,1... | collective-permute-start | bytes 663560 | tf_op jit(solution)/shard_map/ppermute | solution.py:352
  11.3 0.7 %collective-permute-start.3 = (f32[432,128]{1,0:T(8,128)S(1)}, f32[432,128]{1,0:T(8,128)S(1)}, u32[]{:S(2)}, u32[]{:S(2)}) collective-permute-start(f32[432,128]{1,0:T(8,128)S(1)} %get-tuple-element.27), channel_id=1, source_target_pairs={{0,255},{1,0},{2,1},{3,2},{4,3},{5,4},{6,5},{7,6},{8,7},{9,8},{10,... | collective-permute-start | bytes 663560 | tf_op jit(solution)/shard_map/ppermute | solution.py:352
  12.1 5.0 %shard_map.78 = (f32[4608,128]{1,0:T(8,128)S(1)}, bf16[576,1024]{1,0:T(8,128)(2,1)S(1)}, bf16[576,1024]{1,0:T(8,128)(2,1)S(1)}, bf16[512,512]{1,0:T(8,128)(2,1)S...) custom-call(f32[8064,128]{1,0:T(8,128)S(1)} %bitcast.5, f32[32,128]{1,0:T(8,128)S(1)} %bitcast.7, s32[4,128]{1,0:T(4,128)S(1)} %copy-done.8, ...), custom_call_target="tpu_custom_call" | custom-call | flops 500000000 | bytes 4194304 | tf_op jit(solution)/shard_map/pallas_call | solution.py:407
  17.1 1.0 %copy-done.1 = bf16[576,1024]{1,0:T(8,128)(2,1)} copy-done((bf16[576,1024]{1,0:T(8,128)(2,1)}, bf16[576,1024]{1,0:T(8,128)(2,1)S(1)}, u32[]{:S(2)}) %copy-start.1) | copy-done | bytes 1179672
  18.1 1.0 %collective-permute-start = (f32[576,128]{1,0:T(8,128)}, f32[576,128]{1,0:T(8,128)}, u32[]{:S(2)}, u32[]{:S(2)}) collective-permute-start(f32[576,128]{1,0:T(8,128)} %get-tuple-element.21), channel_id=1, source_target_pairs={{0,1},{1,2},{2,3},{3,4},{4,5},{5,6},{6,7},{7,8},{8,9},{9,10},{10,1... | collective-permute-start | bytes 884744 | tf_op jit(solution)/shard_map/ppermute | solution.py:352
  19.1 7.2 %collective-permute-start.1 = (f32[576,128]{1,0:T(8,128)}, f32[576,128]{1,0:T(8,128)}, u32[]{:S(2)}, u32[]{:S(2)}) collective-permute-start(f32[576,128]{1,0:T(8,128)} %get-tuple-element.22), channel_id=1, source_target_pairs={{0,255},{1,0},{2,1},{3,2},{4,3},{5,4},{6,5},{7,6},{8,7},{9,8},{10,... | collective-permute-start | bytes 884744 | tf_op jit(solution)/shard_map/ppermute | solution.py:352
  26.3 0.0 collective-permute-done.2.from_before_ref
  26.3 0.0 collective-permute-done.3.from_after_ref
  26.3 0.0 copy-start.7
  26.3 5.7 %shard_map.79 = (f32[8064,128]{1,0:T(8,128)}, f32[24,128]{1,0:T(8,128)S(1)}) custom-call(s32[16]{0:T(128)S(1)} %bitcast.8, s32[4,128]{1,0:T(4,128)S(1)} %copy-done.6, s32[16,128]{1,0:T(8,128)S(1)} %copy-done.9, f32[3456,128]{1,0:T(8,128)S(1)} %get-tuple-element.23.acc_ref, bf16[432,1024]{1,0:T(8,128)(2,1)S(1)} %get-tuple-element.24.high_ref, ...), custom_call_target="tpu_custom_call" | custom-call | flops 2000000000 | bytes 4194304 | tf_op jit(solution)/shard_map/pallas_call | solution.py:417
  32.1 14.2 %all_to_all.5 = f32[8,3,128]{2,1,0:T(4,128)S(1)} all-to-all(f32[8,3,128]{2,1,0:T(4,128)S(1)} %reshape.26), channel_id=1, replica_groups=mesh['elem'=32,'col'=8] {'col'}, dimensions={0} | all-to-all | bytes 24576 | tf_op jit(solution)/shard_map/all_to_all | solution.py:434
  46.2 0.6 %reshape.27 = f32[1,1,24,128]{3,2,1,0:T(8,128)} reshape(f32[8,3,128]{2,1,0:T(4,128)S(1)} %all_to_all.5) | data formatting | bytes 24576 | tf_op jit(solution)/shard_map/reshape | solution.py:448
  46.9 0.0 collective-permute-done.from_before_ref
  46.9 0.0 collective-permute-done.1.from_after_ref
  46.9 1.3 %copy-done.2 = bf16[576,1024]{1,0:T(8,128)(2,1)S(1)} copy-done((bf16[576,1024]{1,0:T(8,128)(2,1)S(1)}, bf16[576,1024]{1,0:T(8,128)(2,1)}, u32[]{:S(2)}) %copy-start.2) | copy-done | bytes 1179672
  48.1 1.3 %copy-done.4 = bf16[576,1024]{1,0:T(8,128)(2,1)S(1)} copy-done((bf16[576,1024]{1,0:T(8,128)(2,1)S(1)}, bf16[576,1024]{1,0:T(8,128)(2,1)}, u32[]{:S(2)}) %copy-start.4) | copy-done | bytes 1179672
  49.4 5.4 %shard_map.80 = f32[8064,128]{1,0:T(8,128)} custom-call(s32[4,128]{1,0:T(4,128)S(1)} %copy-done.7, f32[4608,128]{1,0:T(8,128)S(1)} %get-tuple-element.17.acc_ref, bf16[576,1024]{1,0:T(8,128)(2,1)S(1)} %copy-done.2, bf16[576,1024]{1,0:T(8,128)(2,1)S(1)} %copy-done.4, bf16[512,512]{1,0:T(8,128)(2,1)S(1)} %get-tuple-element.20.own_ref, ...), custom_call_target="tpu_custom_call", output_to_operand_aliasing={{}: (8, {})} | custom-call | flops 2000000000 | bytes 4194304 | tf_op jit(solution)/shard_map/pallas_call | solution.py:435
  (13 shorter events, 0.0 us)
Async XLA Ops:
  0.6 2.2 %copy-start = (f32[7,72,16,128]{3,2,1,0:T(8,128)S(1)}, f32[7,72,16,128]{3,2,1,0:T(8,128)}, u32[]{:S(2)}) copy-start(f32[7,72,16,128]{3,2,1,0:T(8,128)} %param.6) | copy-start | bytes 12386308
  2.8 0.7 %copy-start.5 = (f32[2,16,128]{2,1,0:T(8,128)S(1)}, f32[2,16,128]{2,1,0:T(8,128)}, u32[]{:S(2)}) copy-start(f32[2,16,128]{2,1,0:T(8,128)} %param.7) | copy-start | bytes 49156
  3.5 0.7 %copy-start.6 = (s32[4,128]{1,0:T(4,128)S(1)}, s32[4,128]{1,0:T(4,128)}, u32[]{:S(2)}) copy-start(s32[4,128]{1,0:T(4,128)} %code_ref.3) | copy-start | bytes 6148
  4.2 0.7 %copy-start.8 = (s32[4,128]{1,0:T(4,128)S(1)}, s32[4,128]{1,0:T(4,128)}, u32[]{:S(2)}) copy-start(s32[4,128]{1,0:T(4,128)} %refs_2_.3) | copy-start | bytes 6148
  8.6 17.7 %copy-start.9 = (s32[16,128]{1,0:T(8,128)S(1)}, s32[16,128]{1,0:T(8,128)}, u32[]{:S(2)}) copy-start(s32[16,128]{1,0:T(8,128)} %mark_ref.1) | copy-start | bytes 24580
  8.6 17.7 %copy-start.10 = (s32[16,1]{0,1:T(1,128)S(1)}, s32[16,1]{0,1:T(1,128)}, u32[]{:S(2)}) copy-start(s32[16,1]{0,1:T(1,128)} %param.10) | copy-start | bytes 196
  8.7 17.7 %collective-permute-start.2 = (f32[432,128]{1,0:T(8,128)S(1)}, f32[432,128]{1,0:T(8,128)S(1)}, u32[]{:S(2)}, u32[]{:S(2)}) collective-permute-start(f32[432,128]{1,0:T(8,128)S(1)} %get-tuple-element.26), channel_id=1, source_target_pairs={{0,1},{1,2},{2,3},{3,4},{4,5},{5,6},{6,7},{7,8},{8,9},{9,10},{10,1... | collective-permute-start | bytes 663560 | tf_op jit(solution)/shard_map/ppermute | solution.py:352
  11.3 15.0 %collective-permute-start.3 = (f32[432,128]{1,0:T(8,128)S(1)}, f32[432,128]{1,0:T(8,128)S(1)}, u32[]{:S(2)}, u32[]{:S(2)}) collective-permute-start(f32[432,128]{1,0:T(8,128)S(1)} %get-tuple-element.27), channel_id=1, source_target_pairs={{0,255},{1,0},{2,1},{3,2},{4,3},{5,4},{6,5},{7,6},{8,7},{9,8},{10,... | collective-permute-start | bytes 663560 | tf_op jit(solution)/shard_map/ppermute | solution.py:352
  17.1 1.0 %copy-start.1 = (bf16[576,1024]{1,0:T(8,128)(2,1)}, bf16[576,1024]{1,0:T(8,128)(2,1)S(1)}, u32[]{:S(2)}) copy-start(bf16[576,1024]{1,0:T(8,128)(2,1)S(1)} %get-tuple-element.18.high_ref) | copy-start | bytes 3538948
  18.1 13.9 %copy-start.3 = (bf16[576,1024]{1,0:T(8,128)(2,1)}, bf16[576,1024]{1,0:T(8,128)(2,1)S(1)}, u32[]{:S(2)}) copy-start(bf16[576,1024]{1,0:T(8,128)(2,1)S(1)} %get-tuple-element.19.low_ref) | copy-start | bytes 3538948
  18.1 28.8 %collective-permute-start = (f32[576,128]{1,0:T(8,128)}, f32[576,128]{1,0:T(8,128)}, u32[]{:S(2)}, u32[]{:S(2)}) collective-permute-start(f32[576,128]{1,0:T(8,128)} %get-tuple-element.21), channel_id=1, source_target_pairs={{0,1},{1,2},{2,3},{3,4},{4,5},{5,6},{6,7},{7,8},{8,9},{9,10},{10,1... | collective-permute-start | bytes 884744 | tf_op jit(solution)/shard_map/ppermute | solution.py:352
  19.1 27.7 %collective-permute-start.1 = (f32[576,128]{1,0:T(8,128)}, f32[576,128]{1,0:T(8,128)}, u32[]{:S(2)}, u32[]{:S(2)}) collective-permute-start(f32[576,128]{1,0:T(8,128)} %get-tuple-element.22), channel_id=1, source_target_pairs={{0,255},{1,0},{2,1},{3,2},{4,3},{5,4},{6,5},{7,6},{8,7},{9,8},{10,... | collective-permute-start | bytes 884744 | tf_op jit(solution)/shard_map/ppermute | solution.py:352
  26.3 20.5 %copy-start.7 = (s32[4,128]{1,0:T(4,128)S(1)}, s32[4,128]{1,0:T(4,128)}, u32[]{:S(2)}) copy-start(s32[4,128]{1,0:T(4,128)} %code_ref.3) | copy-start | bytes 6148
  46.9 1.3 %copy-start.2 = (bf16[576,1024]{1,0:T(8,128)(2,1)S(1)}, bf16[576,1024]{1,0:T(8,128)(2,1)}, u32[]{:S(2)}) copy-start(bf16[576,1024]{1,0:T(8,128)(2,1)} %copy-done.1) | copy-start | bytes 3538948
  48.1 1.3 %copy-start.4 = (bf16[576,1024]{1,0:T(8,128)(2,1)S(1)}, bf16[576,1024]{1,0:T(8,128)(2,1)}, u32[]{:S(2)}) copy-start(bf16[576,1024]{1,0:T(8,128)(2,1)} %copy-done.3) | copy-start | bytes 3538948
where the time goes:
time: 55.2 us; the launch traced here: 54.8 us
  Pallas kernels  19.8 us (36%)
  blocking collectives  14.2 us (26%)
  starting transfers between devices  11.6 us (21%)
  local copies, waits for them, and re-layouts  8.45 us (15%)
  between operations  0.74 us (1%)
    all_to_all x1, blocking collectives, body(): lax.all_to_all(rain.reshape(8, CAP, LANES), 'col', split_axis=0, concat_a...  14.2 us
    ppermute x4, starting transfers between devices, passed_along(): return lax.ppermute(value, axis, pairs)  11.6 us
    unnamed x22, local copies, waits for them, and re-layouts  7.83 us
    pallas_call x1, Pallas kernels, body(): call(third_kernel, [shape(7 * ROWS, LANES), shape(8 * CAP, LANES)], [SM]...  5.7 us
    pallas_call x1, Pallas kernels, body(): call(fourth_kernel, shape(7 * ROWS, LANES), [VM] * 8 + [ANY], ANY, [pltpu...  5.4 us
    pallas_call x1, Pallas kernels, body(): call(lambda *refs: second_kernel(devices, *refs), sizes(n2) + [shape(512,...  4.98 us
    pallas_call x1, Pallas kernels, body(): call(lambda *refs: first_kernel(devices, *refs), sizes(n1) + [shape(256,...  3.74 us
  transfers between devices with their start and end apart: 4, of which 0 were waited for; matrix products, arithmetic and copies ran while one was open for 1% of the time, Pallas kernels for 19%

commit v1 on v0

v1 whole, which is shorter than its diff:
```python
import jax
import jax.numpy as jnp
import numpy as np
from jax import lax
from jax.experimental import pallas as pl
from jax.experimental.pallas import tpu as pltpu
from jax.sharding import PartitionSpec as P

LEV = 72
GROUPS = LEV // 8
ROWS = LEV * 16
LANES = 128
EDGE_POINTS = ((0, 1, 2, 3), (3, 7, 11, 15), (12, 13, 14, 15), (0, 4, 8, 12))
RIM_POINTS = (0, 1, 2, 3, 4, 7, 8, 11, 12, 13, 14, 15)
CORNERS = (0, 3, 12, 15)
SCALE = 0.5 * 0.03
ORDER = (2, 3, 4, 0, 1, 5, 6)
NVAR = 7
LINES = NVAR * GROUPS * 16
CAP = 3
F32 = jnp.float32
BF16 = jnp.bfloat16
VMEM_LIMIT = 20 * 1024 * 1024


def derivative_matrix():
    nodes = np.array([-1.0, -1.0 / np.sqrt(5.0), 1.0 / np.sqrt(5.0), 1.0])
    weights = np.array(
        [1.0 / np.prod([nodes[a] - nodes[b] for b in range(4) if b != a]) for a in range(4)]
    )
    table = np.zeros((4, 4))
    for a in range(4):
        for b in range(4):
            if a != b:
                table[a, b] = weights[b] / weights[a] / (nodes[a] - nodes[b])
        table[a, a] = -table[a].sum()
    return table


DG = derivative_matrix()
EVEN0 = float((DG[0, 0] + DG[0, 3]) / 2)
EVEN1 = float((DG[1, 0] + DG[1, 3]) / 2)
ODD00 = float((DG[0, 0] - DG[0, 3]) / 2)
ODD01 = float((DG[0, 1] - DG[0, 2]) / 2)
ODD10 = float((DG[1, 0] - DG[1, 3]) / 2)
ODD11 = float((DG[1, 1] - DG[1, 2]) / 2)


def derive_fluxes(u0, u1, u2, u3):
    even = (u0 + u3) - (u1 + u2)
    o0 = u0 - u3
    o1 = u1 - u2
    b0 = (ODD00 / EVEN0) * o0 + (ODD01 / EVEN0) * o1
    b1 = (ODD10 / EVEN1) * o0 + (ODD11 / EVEN1) * o1
    return even + b0, even + b1, b1 - even, b0 - even


def derive_again(u0, u1, u2, u3):
    even = (u0 + u3) - (u1 + u2)
    o0 = u0 - u3
    o1 = u1 - u2
    a1 = (EVEN1 / EVEN0) * even
    b0 = (ODD00 / EVEN0) * o0 + (ODD01 / EVEN0) * o1
    b1 = (ODD10 / EVEN0) * o0 + (ODD11 / EVEN0) * o1
    return even + b0, a1 + b1, b1 - a1, b0 - even


def metric_scale(direction, point):
    row = (point // 4, point % 4)[1 - direction]
    return SCALE * EVEN0 * (EVEN0, EVEN1, EVEN1, EVEN0)[row]


def scaled_tendency(u, metric):
    total = [None] * 16
    for b in range(4):
        points = [4 * b + a for a in range(4)]
        flux = derive_fluxes(*[u[p] for p in points])
        for p, value in zip(points, derive_again(*[f * metric(0, p) for f, p in zip(flux, points)])):
            total[p] = value
    for a in range(4):
        points = [a + 4 * b for b in range(4)]
        flux = derive_fluxes(*[u[p] for p in points])
        for p, value in zip(points, derive_again(*[f * metric(1, p) for f, p in zip(flux, points)])):
            total[p] = total[p] + value
    return total


def edge_rows(peer_ref, code_ref, me, devices):
    rows = []
    for k in range(4):
        peer = peer_ref[k : k + 1, :]
        code = code_ref[k : k + 1, :]
        offset = lax.shift_right_logical(peer, 7) - me
        source = lax.shift_right_logical(code, 1) * LANES + lax.bitwise_and(peer, LANES - 1)
        rows.append(
            dict(
                source=source,
                own=offset == 0,
                after=(offset == 1) | (offset == 1 - devices),
                before=(offset == -1) | (offset == devices - 1),
            )
        )
    return rows


def one_hot(mask):
    return jnp.where(mask, 1.0, 0.0).astype(BF16)


def pack_weights(rows, even, hit_ref, less_ref, pack_ref, halo_ref):
    number = lax.broadcasted_iota(jnp.int32, (512, LANES), 0)
    for k, row in enumerate(rows):
        hit_ref[:, k * LANES : (k + 1) * LANES] = one_hot((number == row["source"]) & row["before"])
        less_ref[:, k * LANES : (k + 1) * LANES] = one_hot(number < row["source"])
    met = lax.dot_general(
        jnp.ones((16, 512), BF16), hit_ref[...], (((1,), (1,)), ((), ())), preferred_element_type=F32
    )
    before_slot = jnp.dot(met.astype(BF16), less_ref[...], preferred_element_type=F32)
    lane = lax.broadcasted_iota(jnp.int32, (512, LANES), 1)
    for k in range(4):
        less_ref[:, k * LANES : (k + 1) * LANES] = one_hot(number < lane + k * LANES)
    meets = jnp.concatenate([jnp.where(row["after"], 1.0, 0.0) for row in rows], axis=1)
    after_slot = jnp.dot(
        jnp.broadcast_to(meets, (16, 512)).astype(BF16), less_ref[...], preferred_element_type=F32
    )
    slot = lax.broadcasted_iota(jnp.int32, (64, LANES), 0)
    zero = jnp.zeros((64, LANES), BF16)
    for k, row in enumerate(rows):
        low = slice(k * LANES, (k + 1) * LANES)
        high = slice(512 + k * LANES, 512 + (k + 1) * LANES)
        after = jnp.where(row["after"], after_slot[0:1, low], -1.0).astype(jnp.int32)
        before = jnp.where(row["before"], before_slot[0:1, low], -1.0).astype(jnp.int32)
        near = one_hot(slot == jnp.where(even, after, before))
        far = one_hot(slot == jnp.where(even, before, after))
        pack_ref[0:64, low] = near
        pack_ref[0:64, high] = zero
        pack_ref[64:128, low] = zero
        pack_ref[64:128, high] = near
        pack_ref[128:192, low] = zero
        pack_ref[128:192, high] = far
        pack_ref[192:256, low] = far
        pack_ref[192:256, high] = zero
        for again in (0, 128):
            halo_ref[again : again + 64, low] = near
            halo_ref[again + 64 : again + 128, low] = far
            halo_ref[again : again + 64, high] = far
            halo_ref[again + 64 : again + 128, high] = near


def edges_out(state_ref, metric_ref, pack_ref, acc_ref, high_ref, low_ref, near_ref, far_ref, ready):
    def metric(direction, point):
        row = 8 * (16 * direction + point)
        return metric_ref[row : row + 8, :]

    def group(index, carry):
        base = index * 128
        u = [state_ref[pl.ds(base + p, 8, stride=16), :] for p in range(16)]
        tendency = scaled_tendency(u, metric)
        for p in range(16):
            if p in CORNERS:
                value = u[p]
            elif p in RIM_POINTS:
                value = u[p] + tendency[p]
            else:
                value = u[p] + 2.0 * tendency[p]
            acc_ref[pl.ds(pl.multiple_of(base + 8 * p, 8), 8), :] = value
        top = {p: tendency[p].astype(BF16).astype(F32) for p in RIM_POINTS}
        rest = {p: tendency[p] - top[p] for p in RIM_POINTS}
        rows = pl.ds(pl.multiple_of(index * 16, 16), 16)
        for k in range(4):
            for half in range(2):
                first, second = EDGE_POINTS[k][2 * half : 2 * half + 2]
                place = slice(half * 512 + k * LANES, half * 512 + (k + 1) * LANES)
                high_ref[rows, place] = jnp.concatenate([top[first], top[second]], 0).astype(BF16)
                low_ref[rows, place] = jnp.concatenate([rest[first], rest[second]], 0).astype(BF16)
        return carry

    for var in range(NVAR):
        ready(var)
        lax.fori_loop(var * GROUPS, (var + 1) * GROUPS, group, 0)
    across = (((1,), (1,)), ((), ()))
    packed = lax.dot_general(
        high_ref[...], pack_ref[...], across, preferred_element_type=F32
    ) + lax.dot_general(low_ref[...], pack_ref[...], across, preferred_element_type=F32)
    near_ref[...] = packed[:, :LANES]
    far_ref[...] = packed[:, LANES:]


def first_kernel(devices, state_hbm, metric_hbm, peer_hbm, code_hbm, work_hbm,
                 code_ref, work_ref, own_ref, halo_ref, acc_ref, high_ref, low_ref, near_ref, far_ref,
                 state_ref, metric_ref, scaled_ref, peer_ref, hit_ref, less_ref, pack_ref, sems):
    me = lax.axis_index(("elem", "col"))
    small = [
        pltpu.make_async_copy(source, target, sems.at[NVAR + i])
        for i, (source, target) in enumerate(
            [(peer_hbm, peer_ref), (code_hbm, code_ref), (metric_hbm, metric_ref), (work_hbm, work_ref)]
        )
    ]
    large = [
        pltpu.make_async_copy(
            state_hbm.at[pl.ds(var * ROWS, ROWS)], state_ref.at[pl.ds(i * ROWS, ROWS)], sems.at[i]
        )
        for i, var in enumerate(ORDER)
    ]
    for copy in small + large:
        copy.start()
    small[0].wait()
    small[1].wait()
    rows = edge_rows(peer_ref, code_ref, me, devices)
    pack_weights(rows, lax.rem(me, 2) == 0, hit_ref, less_ref, pack_ref, halo_ref)
    number = lax.broadcasted_iota(jnp.int32, (512, LANES), 0)
    for k, row in enumerate(rows):
        own_ref[:, k * LANES : (k + 1) * LANES] = one_hot((number == row["source"]) & row["own"])
    small[2].wait()
    small[3].wait()
    for i in range(32):
        scaled_ref[8 * i : 8 * i + 8, :] = jnp.broadcast_to(
            metric_scale(i // 16, i % 16) * metric_ref[i : i + 1, :], (8, LANES)
        )
    edges_out(state_ref, scaled_ref, pack_ref, acc_ref, high_ref, low_ref, near_ref, far_ref,
              lambda i: large[i].wait())


def split(value):
    top = value.astype(BF16)
    return top, (value - top.astype(F32)).astype(BF16)


def turned_edges(code_ref):
    return [
        jnp.broadcast_to(lax.bitwise_and(code_ref[k : k + 1, :], 1), (8, LANES)) == 1 for k in range(4)
    ]


def averaged(index, turned, acc_ref, lines_ref):
    base = index * 128
    value = [acc_ref[pl.ds(pl.multiple_of(base + 8 * p, 8), 8), :] for p in range(16)]
    for k in range(4):
        line = []
        for half in range(2):
            place = slice(half * 512 + k * LANES, half * 512 + (k + 1) * LANES)
            for second in range(2):
                rows = pl.ds(pl.multiple_of(index * 16 + 8 * second, 8), 8)
                line.append(lines_ref[rows, place])
        for t in range(4):
            p = EDGE_POINTS[k][t]
            value[p] = value[p] + jnp.where(turned[k], line[3 - t], line[t])
    return value


def second_kernel(code_ref, acc_ref, high_ref, low_ref, own_ref, out_ref, lines_ref):
    for half in range(2):
        place = slice(half * 512, (half + 1) * 512)
        lines_ref[:, place] = jnp.dot(
            high_ref[:, place], own_ref[...], preferred_element_type=F32
        ) + jnp.dot(low_ref[:, place], own_ref[...], preferred_element_type=F32)
    turned = turned_edges(code_ref)

    def group(index, carry):
        for p, value in enumerate(averaged(index, turned, acc_ref, lines_ref)):
            out_ref[pl.ds(pl.multiple_of(index * 128 + 8 * p, 8), 8), :] = value
        return carry

    lax.fori_loop(0, NVAR * GROUPS, group, 0)


def softplus(x):
    tail = jnp.exp(-jnp.abs(x))
    small = tail - 0.5 * tail * tail
    return jnp.maximum(x, 0.0) + jnp.where(tail < 1e-3, small, jnp.log(1.0 + tail))


UNROLL = 8


def physics(dyn_ref, mark_ref):
    work = mark_ref[...]
    marks = [jnp.where(work >= section, 0.3, 0.0) for section in (1, 2, 3)]

    def condense(block, rain):
        base = pl.multiple_of(block * (16 * UNROLL), 16)
        for step in range(UNROLL):
            heat_at = pl.ds(base + 16 * step, 16)
            vapour_at = pl.ds(ROWS + base + 16 * step, 16)
            water_at = pl.ds(2 * ROWS + base + 16 * step, 16)
            heat = dyn_ref[heat_at, :]
            vapour = dyn_ref[vapour_at, :]
            excess = vapour - 0.5 * heat
            total = None
            for mark in marks:
                amount = mark * softplus(excess)
                excess = excess - 1.25 * amount
                total = amount if total is None else total + amount
            dyn_ref[heat_at, :] = heat + 0.5 * total
            dyn_ref[vapour_at, :] = vapour - total
            dyn_ref[water_at, :] = dyn_ref[water_at, :] + total
            rain = rain + total
        return rain

    return lax.fori_loop(0, LEV // UNROLL, condense, jnp.zeros((16, LANES), F32))


def mixed(dyn_ref, out_ref):
    for var in range(3):
        start = var * ROWS

        def at(level, start=start):
            return dyn_ref[pl.ds(start + 16 * level, 16), :]

        upper = here = at(0)
        for level in range(LEV):
            lower = at(min(level + 1, LEV - 1))
            out_ref[pl.ds(start + 16 * level, 16), :] = 0.5 * here + 0.25 * (upper + lower)
            upper, here = here, lower


def by_span(rain):
    point = lax.broadcasted_iota(jnp.int32, (16, LANES), 0)
    eighth = lax.shift_right_logical(lax.broadcasted_iota(jnp.int32, (16, LANES), 1), 3)
    total = None
    for shift in range(16):
        moved = pltpu.roll(rain, 8 * shift, 1) if shift else rain
        kept = jnp.where(point == eighth, moved, 0.0)
        kept = pltpu.roll(kept, 16 - shift, 0) if shift else kept
        total = kept if total is None else total + kept
    return total


def halo_lines(first, count, near_ref, far_ref, halo_ref, lines_ref):
    rows = slice(first * 144, (first + count) * 144)
    lane = lax.broadcasted_iota(jnp.int32, (count * 144, LANES), 1)
    for half in range(2):
        low, high = near_ref[rows, :], far_ref[rows, :]
        if half:
            low, high = high, low
        halo = jnp.concatenate(split(jnp.where(lane < 64, low, high)), axis=1)
        place = slice(half * 512, (half + 1) * 512)
        lines_ref[rows, place] = jnp.dot(halo, halo_ref[:, place], preferred_element_type=F32)


def third_kernel(owner_ref, code_ref, mark_ref, acc_ref, halo_ref, near_ref, far_ref,
                 mixed_ref, rain_ref,
                 lines_ref, dyn_ref, rain_rows, counts):
    halo_lines(0, 3, near_ref, far_ref, halo_ref, lines_ref)
    turned = turned_edges(code_ref)

    def group(index, carry):
        for p, value in enumerate(averaged(index, turned, acc_ref, lines_ref)):
            dyn_ref[pl.ds(index * 128 + p, 8, stride=16), :] = value
        return carry

    lax.fori_loop(0, 3 * GROUPS, group, 0)
    rain = physics(dyn_ref, mark_ref)
    mixed(dyn_ref, mixed_ref)
    rain_rows[...] = by_span(rain) * (1.0 / LEV)
    rain_ref[...] = jnp.zeros_like(rain_ref)
    for owner in range(8):
        counts[owner] = 0
    for span in range(16):
        owner = owner_ref[span]
        rank = counts[owner]
        counts[owner] = rank + 1
        rain_ref[pl.ds(owner * CAP + rank, 1), :] = rain_rows[span : span + 1, :]


def fourth_kernel(code_ref, acc_ref, halo_ref, near_ref, far_ref, mixed_ref, state_out,
                  lines_ref, dyn_ref, sems):
    def leave(i, source, start):
        return pltpu.make_async_copy(
            source.at[pl.ds(start, ROWS)], state_out.at[pl.ds(ORDER[i] * ROWS, ROWS)], sems.at[i]
        )

    copies = [leave(i, mixed_ref, i * ROWS) for i in range(3)]
    for copy in copies:
        copy.start()
    halo_lines(3, NVAR - 3, near_ref, far_ref, halo_ref, lines_ref)
    turned = turned_edges(code_ref)

    def group(index, carry):
        for p, value in enumerate(averaged(index, turned, acc_ref, lines_ref)):
            dyn_ref[pl.ds(index * 128 + p, 8, stride=16), :] = value
        return carry

    for i in range(3, NVAR):
        lax.fori_loop(i * GROUPS, (i + 1) * GROUPS, group, 0)
        copies.append(leave(i, dyn_ref, i * ROWS))
        copies[-1].start()
    for copy in copies:
        copy.wait()


def fifth_kernel(all_ref, rain_ref):
    me = lax.axis_index("col")
    for source in range(8):
        rain_ref[CAP * source : CAP * (source + 1), :] = all_ref[pl.ds(8 * CAP * source + CAP * me, CAP), :]


def swapped(value, axes, partner):
    count = lax.axis_size(axes)
    return lax.ppermute(value, axes, [(source, partner(source, count)) for source in range(count)])


def near_partner(source, count):
    return source + 1 if source % 2 == 0 else source - 1


def far_partner(source, count):
    return (source - 1) % count if source % 2 == 0 else (source + 1) % count


VM = pl.BlockSpec(memory_space=pltpu.VMEM)
SM = pl.BlockSpec(memory_space=pltpu.SMEM)
HB = pl.BlockSpec(memory_space=pltpu.HBM)


def shape(*sizes, dtype=F32):
    return jax.ShapeDtypeStruct(sizes, dtype)


def call(kernel, out, ins, outs, scratch, cost, **more):
    return pl.pallas_call(
        kernel,
        out_shape=out,
        in_specs=ins,
        out_specs=outs,
        scratch_shapes=scratch,
        cost_estimate=pl.CostEstimate(flops=cost, bytes_accessed=4 << 20, transcendentals=0),
        compiler_params=pltpu.CompilerParams(vmem_limit_bytes=VMEM_LIMIT),
        **more,
    )


def in_hbm(value):
    return pltpu.with_memory_space_constraint(value, pltpu.HBM)


def body(state, metric, edge_peer, edge_code, span_owner, work_class):
    axes = ("elem", "col")
    devices = lax.axis_size(axes)
    state = state.reshape(NVAR * ROWS, LANES)
    metric = metric.reshape(32, LANES)
    owner = span_owner.reshape(16)
    code, work, own, halo, acc, high, low, near, far = call(
        lambda *refs: first_kernel(devices, *refs),
        [
            shape(4, LANES, dtype=jnp.int32),
            shape(16, LANES, dtype=jnp.int32),
            shape(512, 512, dtype=BF16),
            shape(256, 1024, dtype=BF16),
            shape(NVAR * ROWS, LANES),
            shape(LINES, 1024, dtype=BF16),
            shape(LINES, 1024, dtype=BF16),
            shape(LINES, LANES),
            shape(LINES, LANES),
        ],
        [HB] * 5,
        [VM] * 9,
        [
            pltpu.VMEM((NVAR * ROWS, LANES), F32),
            pltpu.VMEM((32, LANES), F32),
            pltpu.VMEM((256, LANES), F32),
            pltpu.VMEM((4, LANES), jnp.int32),
            pltpu.VMEM((512, 512), BF16),
            pltpu.VMEM((512, 512), BF16),
            pltpu.VMEM((256, 1024), BF16),
            pltpu.SemaphoreType.DMA((NVAR + 4,)),
        ],
        2_000_000_000,
    )(in_hbm(state), in_hbm(metric), in_hbm(edge_peer), in_hbm(edge_code), in_hbm(work_class))
    from_far = swapped(far, axes, far_partner)
    acc = call(
        second_kernel,
        shape(NVAR * ROWS, LANES),
        [VM] * 5,
        VM,
        [pltpu.VMEM((LINES, 1024), F32)],
        4_000_000_000,
    )(code, acc, high, low, own)
    near, acc = lax.optimization_barrier((near, acc))
    from_near = swapped(near, axes, near_partner)
    mixed1, rain = call(
        third_kernel,
        [shape(3 * ROWS, LANES), shape(8 * CAP, LANES)],
        [SM] + [VM] * 6,
        [VM, VM],
        [
            pltpu.VMEM((LINES, 1024), F32),
            pltpu.VMEM((3 * ROWS, LANES), F32),
            pltpu.VMEM((16, LANES), F32),
            pltpu.SMEM((8,), jnp.int32),
        ],
        2_000_000_000,
    )(owner, code, work, acc, halo, from_near, from_far)
    rain = lax.all_to_all(rain.reshape(8, CAP, LANES), "col", split_axis=0, concat_axis=0, tiled=True)
    new_state = call(
        fourth_kernel,
        shape(NVAR * ROWS, LANES),
        [VM] * 6,
        HB,
        [
            pltpu.VMEM((LINES, 1024), F32),
            pltpu.VMEM((NVAR * ROWS, LANES), F32),
            pltpu.SemaphoreType.DMA((NVAR,)),
        ],
        10_000_000_000,
    )(code, acc, halo, from_near, from_far, mixed1)
    new_state, rain = lax.optimization_barrier((new_state, rain))
    return new_state.reshape(NVAR, LEV, 16, LANES), rain.reshape(1, 1, 8 * CAP, LANES)


def solution(mesh):
    placed = (
        P(None, None, None, ("elem", "col")),
        P(None, None, ("elem", "col")),
        P(None, ("elem", "col")),
        P(None, ("elem", "col")),
        P(("elem", "col"), None),
        P(None, ("elem", "col")),
    )
    return jax.shard_map(
        body,
        mesh=mesh,
        in_specs=placed,
        out_specs=(P(None, None, None, ("elem", "col")), P("elem", "col", None, None)),
        check_vma=False,
    )
```

time: 55.2 us -> 38.6 us (0.70)
  blocking collectives: 14.2 us -> 0 us
  starting transfers between devices: 11.6 us -> 17 us
  local copies, waits for them, and re-layouts: 8.45 us -> 3.39 us
  Pallas kernels: 19.8 us -> 15.6 us
  waiting for transfers between devices: 0.01 us -> 1.75 us
    all_to_all x1 -> x0, blocking collectives: 14.2 us -> none  [body(): lax.all_to_all(rain.reshape(8, CAP, LANES), 'col', split_axis=0, concat_a...]
    unnamed x22 -> x6, local copies, waits for them, and re-layouts: 7.83 us -> 2.18 us
    all_to_all x0 -> x1, starting transfers between devices: none -> 5.4 us  [body(): lax.all_to_all(rain.reshape(8, CAP, LANES), 'col', split_axis=0, concat_a...]
    pallas_call x4, Pallas kernels: 19.8 us -> 15.6 us  [the longest x1 6.97 us: body(): call(lambda *refs: first_kernel(devices, *refs), [shape(4, LANES, dtype=j...]
    ppermute x4 -> x2, waiting for transfers between devices: 0.01 us -> 1.52 us  [swapped(): lax.ppermute(value, axes, [(source, partner(source, count)) for source in...]
    reshape x1, local copies, waits for them, and re-layouts: 0.01 us -> 0.6 us  [body(): rain.reshape(8, CAP, LANES)]
    ppermute x4 -> x2, starting transfers between devices: 11.6 us -> 11.6 us  [swapped(): lax.ppermute(value, axes, [(source, partner(source, count)) for source in...]
  transfers between devices with their start and end apart: 4 -> 3, of which waited for: 0 -> 2; matrix products, arithmetic and copies ran while one was open for 1% -> 0% of each run, Pallas kernels for 19% -> 14%
where the time goes in v1:
time: 38.6 us; the launch traced here: 38.4 us
  starting transfers between devices  17 us (44%)
  Pallas kernels  15.6 us (40%)
  local copies, waits for them, and re-layouts  3.39 us (9%)
  waiting for transfers between devices  1.75 us (5%)
  between operations  0.68 us (2%)
    ppermute x2, starting transfers between devices, swapped(): lax.ppermute(value, axes, [(source, partner(source, count)) for source in...  11.6 us
    pallas_call x1, Pallas kernels, body(): call(lambda *refs: first_kernel(devices, *refs), [shape(4, LANES, dtype=j...  6.97 us
    all_to_all x1, starting transfers between devices, body(): lax.all_to_all(rain.reshape(8, CAP, LANES), 'col', split_axis=0, concat_a...  5.4 us
    pallas_call x1, Pallas kernels, body(): call(third_kernel, [shape(3 * ROWS, LANES), shape(8 * CAP, LANES)], [SM]...  3.36 us
    pallas_call x1, Pallas kernels, body(): call(second_kernel, shape(NVAR * ROWS, LANES), [VM] * 5, VM, [pltpu.VMEM(...  2.98 us
    pallas_call x1, Pallas kernels, body(): call(fourth_kernel, shape(NVAR * ROWS, LANES), [VM] * 6, HB, [pltpu.VMEM(...  2.27 us
    unnamed x6, local copies, waits for them, and re-layouts  2.18 us
    ppermute x2, waiting for transfers between devices, swapped(): lax.ppermute(value, axes, [(source, partner(source, count)) for source in...  1.52 us
  transfers between devices with their start and end apart: 3, of which 2 were waited for; matrix products, arithmetic and copies ran while one was open for 0% of the time, Pallas kernels for 14%

profile of v1, /device:TPU:1, one launch (start us, length us, event | category | flops | bytes accessed | tf_op | source)
XLA Modules:
  0.0 38.4 jit_solution(8947563254947213200)
XLA Ops:
  0.6 7.0 %shard_map.77 = (s32[4,128]{1,0:T(4,128)S(1)}, s32[16,128]{1,0:T(8,128)S(1)}, bf16[512,512]{1,0:T(8,128)(2,1)S(1)}, bf16[256,1024]{1,0:T(8,128)(2,1)S(1)}, f32[8...) custom-call(f32[8064,128]{1,0:T(8,128)} %bitcast.5, ...), custom_call_target="tpu_custom_call" | custom-call | flops 2000000000 | bytes 4194304 | tf_op jit(solution)/shard_map/pallas_call | solution.py:443
  7.6 2.7 %collective-permute-start.1 = (f32[1008,128]{1,0:T(8,128)S(1)}, f32[1008,128]{1,0:T(8,128)S(1)}, u32[]{:S(2)}, u32[]{:S(2)}) collective-permute-start(f32[1008,128]{1,0:T(8,128)S(1)} %get-tuple-element.26), channel_id=1, source_target_pairs={{0,255},{1,2},{2,1},{3,4},{4,3},{5,6},{6,5},{7,8},{8,7},{9,10},{10... | collective-permute-start | bytes 1548296 | tf_op jit(solution)/shard_map/ppermute | solution.py:400
  10.3 0.0 copy-start
  10.3 3.0 %shard_map.78.acc_ref = f32[8064,128]{1,0:T(8,128)S(1)} custom-call(s32[4,128]{1,0:T(4,128)S(1)} %get-tuple-element.17.code_ref, f32[8064,128]{1,0:T(8,128)S(1)} %get-tuple-element.19.acc_ref, bf16[1008,1024]{1,0:T(8,128)(2,1)S(1)} %get-tuple-element.20.high_ref, bf16[1008,1024]{1,0:T(8,128)(2,1)S(1)} %get-tuple-element.21.low_ref, ...), custom_call_target="tpu_custom_call" | custom-call | flops 4000000000 | bytes 4194304 | tf_op jit(solution)/shard_map/pallas_call | solution.py:471
  13.3 0.0 copy-start.1
  13.3 8.9 %collective-permute-start = (f32[1008,128]{1,0:T(8,128)S(1)}, f32[1008,128]{1,0:T(8,128)S(1)}, u32[]{:S(2)}, u32[]{:S(2)}) collective-permute-start(f32[1008,128]{1,0:T(8,128)S(1)} %get-tuple-element.25), channel_id=1, source_target_pairs={{0,1},{1,0},{2,3},{3,2},{4,5},{5,4},{6,7},{7,6},{8,9},{9,8},{10,11... | collective-permute-start | bytes 1548296 | tf_op jit(solution)/shard_map/ppermute | solution.py:400
  22.2 0.0 collective-permute-done.1.far_ref
  22.2 1.5 %collective-permute-done.near_ref = f32[1008,128]{1,0:T(8,128)S(1)} collective-permute-done((f32[1008,128]{1,0:T(8,128)S(1)}, f32[1008,128]{1,0:T(8,128)S(1)}, u32[]{:S(2)}, u32[]{:S(2)}) %collective-permute-start) | collective-permute-done | bytes 516128 | tf_op jit(solution)/shard_map/ppermute | solution.py:400
  23.8 0.0 copy-done
  23.8 3.4 %shard_map.79 = (f32[3456,128]{1,0:T(8,128)S(1)}, f32[24,128]{1,0:T(8,128)S(1)}) custom-call(s32[16]{0:T(128)S(1)} %bitcast.4, s32[4,128]{1,0:T(4,128)S(1)} %get-tuple-element.17.code_ref, s32[16,128]{1,0:T(8,128)S(1)} %get-tuple-element.27.mark_ref, f32[8064,128]{1,0:T(8,128)S(1)} %shard_map.78.acc_ref, bf16[256,1024]{1,0:T(8,128)(2,1)S(1)} %get-tuple-element.24.halo_ref, ...), custom_call_target="tpu_custom_call" | custom-call | flops 2000000000 | bytes 4194304 | tf_op jit(solution)/shard_map/pallas_call | solution.py:481
  27.1 0.0 copy-done.1
  27.1 0.6 %reshape.25 = f32[8,3,128]{2,1,0:T(4,128)} reshape(f32[24,128]{1,0:T(8,128)S(1)} %get-tuple-element.29) | data formatting | bytes 24576 | tf_op jit(solution)/shard_map/reshape | solution.py:494
  27.7 5.4 %all-to-all-start = ((f32[8,3,128]{2,1,0:T(4,128)}), f32[8,3,128]{2,1,0:T(4,128)S(1)}, u32[]{:S(2)}, u32[]{:S(2)}) async-start(f32[8,3,128]{2,1,0:T(4,128)} %reshape.25), calls=%async_computation | async-start | bytes 32768 | tf_op jit(solution)/shard_map/all_to_all | solution.py:494
  33.1 0.0 copy-start.2
  33.1 2.2 %copy-done.2 = f32[8064,128]{1,0:T(8,128)S(1)} copy-done((f32[8064,128]{1,0:T(8,128)S(1)}, f32[8064,128]{1,0:T(8,128)}, u32[]{:S(2)}) %copy-start.2) | copy-done | bytes 4128792
  35.3 2.3 %shard_map.80 = f32[8064,128]{1,0:T(8,128)} custom-call(s32[4,128]{1,0:T(4,128)S(1)} %get-tuple-element.17.code_ref, f32[8064,128]{1,0:T(8,128)S(1)} %copy-done.2, bf16[256,1024]{1,0:T(8,128)(2,1)S(1)} %get-tuple-element.24.halo_ref, f32[1008,128]{1,0:T(8,128)S(1)} %collective-permute-done.near_ref, f32[1008,128]{1,0:T(8,128)S(1)} %collective-permute-done.1.far_ref, ...), custom_call_target="tpu_custom_call" | custom-call | flops 10000000000 | bytes 4194304 | tf_op jit(solution)/shard_map/pallas_call | solution.py:495
  37.6 0.2 all-to-all-done
  37.8 0.6 %reshape.27 = f32[1,1,24,128]{3,2,1,0:T(8,128)} reshape(f32[8,3,128]{2,1,0:T(4,128)S(1)} %all-to-all-done) | data formatting | bytes 24576 | tf_op jit(solution)/shard_map/reshape | solution.py:508
Async XLA Ops:
  7.6 14.6 %collective-permute-start.1 = (f32[1008,128]{1,0:T(8,128)S(1)}, f32[1008,128]{1,0:T(8,128)S(1)}, u32[]{:S(2)}, u32[]{:S(2)}) collective-permute-start(f32[1008,128]{1,0:T(8,128)S(1)} %get-tuple-element.26), channel_id=1, source_target_pairs={{0,255},{1,2},{2,1},{3,4},{4,3},{5,6},{6,5},{7,8},{8,7},{9,10},{10... | collective-permute-start | bytes 1548296 | tf_op jit(solution)/shard_map/ppermute | solution.py:400
  10.3 13.5 %copy-start = (s32[16,1]{0,1:T(1,128)S(1)}, s32[16,1]{0,1:T(1,128)}, u32[]{:S(2)}) copy-start(s32[16,1]{0,1:T(1,128)} %param.10) | copy-start | bytes 196
  13.3 13.8 %copy-start.1 = (f32[8064,128]{1,0:T(8,128)}, f32[8064,128]{1,0:T(8,128)S(1)}, u32[]{:S(2)}) copy-start(f32[8064,128]{1,0:T(8,128)S(1)} %shard_map.78.acc_ref) | copy-start | bytes 12386308
  13.3 10.5 %collective-permute-start = (f32[1008,128]{1,0:T(8,128)S(1)}, f32[1008,128]{1,0:T(8,128)S(1)}, u32[]{:S(2)}, u32[]{:S(2)}) collective-permute-start(f32[1008,128]{1,0:T(8,128)S(1)} %get-tuple-element.25), channel_id=1, source_target_pairs={{0,1},{1,0},{2,3},{3,2},{4,5},{5,4},{6,7},{7,6},{8,9},{9,8},{10,11... | collective-permute-start | bytes 1548296 | tf_op jit(solution)/shard_map/ppermute | solution.py:400
  27.7 10.1 %all-to-all-start = ((f32[8,3,128]{2,1,0:T(4,128)}), f32[8,3,128]{2,1,0:T(4,128)S(1)}, u32[]{:S(2)}, u32[]{:S(2)}) async-start(f32[8,3,128]{2,1,0:T(4,128)} %reshape.25), calls=%async_computation | async-start | bytes 32768 | tf_op jit(solution)/shard_map/all_to_all | solution.py:494
  33.1 2.2 %copy-start.2 = (f32[8064,128]{1,0:T(8,128)S(1)}, f32[8064,128]{1,0:T(8,128)}, u32[]{:S(2)}) copy-start(f32[8064,128]{1,0:T(8,128)} %copy-done.1) | copy-start | bytes 12386308

commit v2 on v1

v2 whole, which is shorter than its diff:
```python
import jax
import jax.numpy as jnp
import numpy as np
from jax import lax
from jax.experimental import pallas as pl
from jax.experimental.pallas import tpu as pltpu
from jax.sharding import PartitionSpec as P

LEV = 72
GROUPS = LEV // 8
ROWS = LEV * 16
LANES = 128
EDGE_POINTS = ((0, 1, 2, 3), (3, 7, 11, 15), (12, 13, 14, 15), (0, 4, 8, 12))
RIM_POINTS = (0, 1, 2, 3, 4, 7, 8, 11, 12, 13, 14, 15)
CORNERS = (0, 3, 12, 15)
SCALE = 0.5 * 0.03
ORDER = (2, 3, 4, 0, 1, 5, 6)
NVAR = 7
AHEAD = 3
LINES = NVAR * GROUPS * 16
CAP = 3
F32 = jnp.float32
BF16 = jnp.bfloat16
VMEM_LIMIT = 20 * 1024 * 1024


def derivative_matrix():
    nodes = np.array([-1.0, -1.0 / np.sqrt(5.0), 1.0 / np.sqrt(5.0), 1.0])
    weights = np.array(
        [1.0 / np.prod([nodes[a] - nodes[b] for b in range(4) if b != a]) for a in range(4)]
    )
    table = np.zeros((4, 4))
    for a in range(4):
        for b in range(4):
            if a != b:
                table[a, b] = weights[b] / weights[a] / (nodes[a] - nodes[b])
        table[a, a] = -table[a].sum()
    return table


DG = derivative_matrix()
EVEN0 = float((DG[0, 0] + DG[0, 3]) / 2)
EVEN1 = float((DG[1, 0] + DG[1, 3]) / 2)
ODD00 = float((DG[0, 0] - DG[0, 3]) / 2)
ODD01 = float((DG[0, 1] - DG[0, 2]) / 2)
ODD10 = float((DG[1, 0] - DG[1, 3]) / 2)
ODD11 = float((DG[1, 1] - DG[1, 2]) / 2)


def derive_fluxes(u0, u1, u2, u3):
    even = (u0 + u3) - (u1 + u2)
    o0 = u0 - u3
    o1 = u1 - u2
    b0 = (ODD00 / EVEN0) * o0 + (ODD01 / EVEN0) * o1
    b1 = (ODD10 / EVEN1) * o0 + (ODD11 / EVEN1) * o1
    return even + b0, even + b1, b1 - even, b0 - even


def derive_again(u0, u1, u2, u3):
    even = (u0 + u3) - (u1 + u2)
    o0 = u0 - u3
    o1 = u1 - u2
    a1 = (EVEN1 / EVEN0) * even
    b0 = (ODD00 / EVEN0) * o0 + (ODD01 / EVEN0) * o1
    b1 = (ODD10 / EVEN0) * o0 + (ODD11 / EVEN0) * o1
    return even + b0, a1 + b1, b1 - a1, b0 - even


def metric_scale(direction, point):
    row = (point // 4, point % 4)[1 - direction]
    return SCALE * EVEN0 * (EVEN0, EVEN1, EVEN1, EVEN0)[row]


def scaled_tendency(u, metric):
    total = [None] * 16
    for b in range(4):
        points = [4 * b + a for a in range(4)]
        flux = derive_fluxes(*[u[p] for p in points])
        for p, value in zip(points, derive_again(*[f * metric(0, p) for f, p in zip(flux, points)])):
            total[p] = value
    for a in range(4):
        points = [a + 4 * b for b in range(4)]
        flux = derive_fluxes(*[u[p] for p in points])
        for p, value in zip(points, derive_again(*[f * metric(1, p) for f, p in zip(flux, points)])):
            total[p] = total[p] + value
    return total


def edge_rows(peer_ref, code_ref, me, devices):
    rows = []
    for k in range(4):
        peer = peer_ref[k : k + 1, :]
        code = code_ref[k : k + 1, :]
        offset = lax.shift_right_logical(peer, 7) - me
        source = lax.shift_right_logical(code, 1) * LANES + lax.bitwise_and(peer, LANES - 1)
        rows.append(
            dict(
                source=source,
                own=offset == 0,
                after=(offset == 1) | (offset == 1 - devices),
                before=(offset == -1) | (offset == devices - 1),
            )
        )
    return rows


def one_hot(mask):
    return jnp.where(mask, 1.0, 0.0).astype(BF16)


def slots_of(rows, even, hit_ref, less_ref, pack_ref, slots_ref):
    number = lax.broadcasted_iota(jnp.int32, (512, LANES), 0)
    for k, row in enumerate(rows):
        low = slice(k * LANES, (k + 1) * LANES)
        hit_ref[:, low] = one_hot(number == jnp.where(row["before"], row["source"], -1))
        less_ref[:, low] = one_hot(number < row["source"])
    met = lax.dot_general(
        jnp.ones((16, 512), BF16), hit_ref[...], (((1,), (1,)), ((), ())), preferred_element_type=F32
    )
    before_slot = jnp.dot(met.astype(BF16), less_ref[...], preferred_element_type=F32)
    lower = one_hot(
        lax.broadcasted_iota(jnp.int32, (LANES, LANES), 0) < lax.broadcasted_iota(jnp.int32, (LANES, LANES), 1)
    )
    passed = jnp.zeros((1, 1), F32)
    slot = lax.broadcasted_iota(jnp.int32, (64, LANES), 0)
    for k, row in enumerate(rows):
        low = slice(k * LANES, (k + 1) * LANES)
        meets = jnp.where(row["after"], 1.0, 0.0)
        after_slot = passed + jnp.dot(
            jnp.broadcast_to(meets, (16, LANES)).astype(BF16), lower, preferred_element_type=F32
        )
        passed = passed + jnp.sum(meets, axis=1, keepdims=True)
        after = jnp.where(row["after"], after_slot[0:1, :], -1.0).astype(jnp.int32)
        before = jnp.where(row["before"], before_slot[0:1, low], -1.0).astype(jnp.int32)
        near = jnp.where(even, after, before)
        far = jnp.where(even, before, after)
        slots_ref[0:1, low] = near
        slots_ref[1:2, low] = far
        high = slice(512 + k * LANES, 512 + (k + 1) * LANES)
        pack_ref[0:64, low] = pack_ref[64:128, high] = one_hot(slot == near)
        pack_ref[128:192, high] = pack_ref[192:256, low] = one_hot(slot == far)
        pack_ref[0:64, high] = pack_ref[64:128, low] = jnp.zeros((64, LANES), BF16)
        pack_ref[128:192, low] = pack_ref[192:256, high] = jnp.zeros((64, LANES), BF16)

def place_weights(rows, slots_ref, own_ref, halo_ref):
    number = lax.broadcasted_iota(jnp.int32, (512, LANES), 0)
    slot = lax.broadcasted_iota(jnp.int32, (64, LANES), 0)
    for k, row in enumerate(rows):
        low = slice(k * LANES, (k + 1) * LANES)
        high = slice(512 + k * LANES, 512 + (k + 1) * LANES)
        own_ref[:, low] = one_hot(number == jnp.where(row["own"], row["source"], -1))
        near = one_hot(slot == slots_ref[0:1, low])
        far = one_hot(slot == slots_ref[1:2, low])
        for again in (0, 128):
            halo_ref[again : again + 64, low] = near
            halo_ref[again + 64 : again + 128, low] = far
            halo_ref[again : again + 64, high] = far
            halo_ref[again + 64 : again + 128, high] = near


def split(value):
    top = value.astype(BF16)
    return top, (value - top.astype(F32)).astype(BF16)


def edges_out(state_ref, metric_ref, pack_ref, acc_ref, high_ref, low_ref, near_ref, far_refs, ready):
    flat = state_ref.reshape(2 * NVAR * LEV * 8, LANES)

    def metric(direction, point):
        row = 8 * (16 * direction + point)
        return metric_ref[row : row + 8, :]

    def group(index, carry):
        base = index * 64
        u = [
            flat[pl.ds(base + (p // 8) * (NVAR * LEV * 8) + p % 8, 8, stride=8), :] for p in range(16)
        ]
        tendency = scaled_tendency(u, metric)
        for p in range(16):
            if p in CORNERS:
                value = u[p]
            elif p in RIM_POINTS:
                value = u[p] + tendency[p]
            else:
                value = u[p] + 2.0 * tendency[p]
            acc_ref[pl.ds(pl.multiple_of(index * 128 + 8 * p, 8), 8), :] = value
        rows = pl.ds(pl.multiple_of(index * 16, 16), 16)
        for k in range(4):
            for half in range(2):
                first, second = EDGE_POINTS[k][2 * half : 2 * half + 2]
                place = slice(half * 512 + k * LANES, half * 512 + (k + 1) * LANES)
                top, rest = split(jnp.concatenate([tendency[first], tendency[second]], 0))
                high_ref[rows, place] = top
                low_ref[rows, place] = rest
        return carry

    def variable(var, carry):
        ready(var)
        return lax.fori_loop(var * GROUPS, (var + 1) * GROUPS, group, carry)

    lax.fori_loop(0, NVAR, variable, 0)
    across = (((1,), (1,)), ((), ()))
    packed = lax.dot_general(
        high_ref[...], pack_ref[...], across, preferred_element_type=F32
    ) + lax.dot_general(low_ref[...], pack_ref[...], across, preferred_element_type=F32)
    near_ref[...] = packed[:, :LANES]
    far_refs[0][...] = packed[: 3 * 144, LANES:]
    far_refs[1][...] = packed[3 * 144 :, LANES:]


def first_kernel(devices, state_hbm, metric_hbm, peer_hbm, code_hbm, work_hbm,
                 peer_ref, code_ref, work_ref, slots_ref, acc_ref, high_ref, low_ref,
                 near_ref, far0_ref, far1_ref, state_ref, metric_ref, scaled_ref, hit_ref, less_ref, pack_ref, small_sems, sems):
    me = lax.axis_index(("elem", "col"))
    small = [
        pltpu.make_async_copy(source, target, small_sems.at[i])
        for i, (source, target) in enumerate(
            [(peer_hbm, peer_ref), (code_hbm, code_ref), (metric_hbm, metric_ref), (work_hbm, work_ref)]
        )
    ]

    def half_of(i, half):
        var = jnp.where(i < 3, i + 2, jnp.where(i < 5, i - 3, i))
        return pltpu.make_async_copy(
            state_hbm.at[pl.ds(var * LEV, LEV), pl.ds(8 * half, 8), :],
            state_ref.at[half, pl.ds(i * LEV, LEV)],
            sems.at[i, half],
        )

    def fetch(i):
        for half in range(2):
            half_of(i, half).start()

    for copy in small:
        copy.start()
    fetch(0)
    fetch(1)
    small[0].wait()
    small[1].wait()
    rows = edge_rows(peer_ref, code_ref, me, devices)
    slots_of(rows, lax.rem(me, 2) == 0, hit_ref, less_ref, pack_ref, slots_ref)
    small[2].wait()
    small[3].wait()
    for i in range(32):
        scaled_ref[8 * i : 8 * i + 8, :] = jnp.broadcast_to(
            metric_scale(i // 16, i % 16) * metric_ref[i : i + 1, :], (8, LANES)
        )

    def ready(i):
        for half in range(2):
            half_of(i, half).wait()

        @pl.when(i + AHEAD < NVAR)
        def _():
            fetch(i + AHEAD)

    for i in range(2, AHEAD):
        fetch(i)
    edges_out(state_ref, scaled_ref, pack_ref, acc_ref, high_ref, low_ref,
              near_ref, (far0_ref, far1_ref), ready)


def turned_edges(code_ref):
    return [
        jnp.broadcast_to(lax.bitwise_and(code_ref[k : k + 1, :], 1), (8, LANES)) == 1 for k in range(4)
    ]


def averaged(index, line_index, turned, acc_ref, lines_ref):
    base = index * 128
    value = [acc_ref[pl.ds(pl.multiple_of(base + 8 * p, 8), 8), :] for p in range(16)]
    for k in range(4):
        line = []
        for half in range(2):
            place = slice(half * 512 + k * LANES, half * 512 + (k + 1) * LANES)
            for second in range(2):
                rows = pl.ds(pl.multiple_of(line_index * 16 + 8 * second, 8), 8)
                line.append(lines_ref[rows, place])
        for t in range(4):
            p = EDGE_POINTS[k][t]
            value[p] = value[p] + jnp.where(turned[k], line[3 - t], line[t])
    return value


def second_kernel(devices, peer_ref, code_ref, slots_ref, acc_ref, high_ref, low_ref,
                  halo_ref, first_ref, rest_ref, own_ref, lines_ref):
    me = lax.axis_index(("elem", "col"))
    place_weights(edge_rows(peer_ref, code_ref, me, devices), slots_ref, own_ref, halo_ref)

    for half in range(2):
        place = slice(half * 512, (half + 1) * 512)
        lines_ref[:, place] = jnp.dot(
            high_ref[:, place], own_ref[...], preferred_element_type=F32
        ) + jnp.dot(low_ref[:, place], own_ref[...], preferred_element_type=F32)
    turned = turned_edges(code_ref)

    def group_into(out_ref, skipped):
        def group(index, carry):
            for p, value in enumerate(averaged(index, index, turned, acc_ref, lines_ref)):
                out_ref[pl.ds(pl.multiple_of((index - skipped * GROUPS) * 128 + 8 * p, 8), 8), :] = value
            return carry

        return group

    lax.fori_loop(0, 3 * GROUPS, group_into(first_ref, 0), 0)
    lax.fori_loop(3 * GROUPS, NVAR * GROUPS, group_into(rest_ref, 3), 0)


LOG2E = float(np.log2(np.e))


def softplus2(y):
    tail = jnp.exp2(jnp.minimum(y, -y))
    small = tail * (LOG2E - (0.5 * LOG2E) * tail)
    return jnp.maximum(y, 0.0) + jnp.where(tail < 1e-3, small, jnp.log2(1.0 + tail))


UNROLL = 8


def level(half, var, number):
    return pl.ds((half * 3 + var) * (LEV * 8) + number, 8)


def physics(dyn_ref, mark_ref):
    work = [mark_ref[8 * half : 8 * half + 8, :] for half in range(2)]
    marks = [[jnp.where(w >= section, 1.0, 0.0) for section in (1, 2, 3)] for w in work]

    def condense(block, rain):
        base = pl.multiple_of(block * (8 * UNROLL), 8)
        rain = list(rain)
        for step in range(UNROLL):
            for half in range(2):
                heat_at, vapour_at, water_at = [level(half, var, base + 8 * step) for var in range(3)]
                heat = dyn_ref[heat_at, :]
                vapour = dyn_ref[vapour_at, :]
                excess = LOG2E * vapour - (0.5 * LOG2E) * heat
                total = None
                for mark in marks[half]:
                    amount = mark * softplus2(excess)
                    excess = excess - (1.25 * 0.3) * amount
                    total = amount if total is None else total + amount
                total = (0.3 / LOG2E) * total
                dyn_ref[heat_at, :] = heat + 0.5 * total
                dyn_ref[vapour_at, :] = vapour - total
                dyn_ref[water_at, :] = dyn_ref[water_at, :] + total
                rain[half] = rain[half] + total
        return tuple(rain)

    zero = jnp.zeros((8, LANES), F32)
    return jnp.concatenate(lax.fori_loop(0, LEV // UNROLL, condense, (zero, zero)), axis=0)


def mixed(var, dyn_ref, out_ref):
    for half in range(2):

        def at(number, half=half):
            return dyn_ref[level(half, var, 8 * number), :]

        here = at(0)
        above = here + here
        for number in range(LEV):
            lower = at(min(number + 1, LEV - 1))
            below = here + lower
            out_ref[level(half, var, 8 * number), :] = 0.25 * (above + below)
            here, above = lower, below


def by_span(rain):
    point = lax.broadcasted_iota(jnp.int32, (16, LANES), 0)
    eighth = lax.shift_right_logical(lax.broadcasted_iota(jnp.int32, (16, LANES), 1), 3)
    total = None
    for shift in range(16):
        moved = pltpu.roll(rain, 8 * shift, 1) if shift else rain
        kept = jnp.where(point == eighth, moved, 0.0)
        kept = pltpu.roll(kept, 16 - shift, 0) if shift else kept
        total = kept if total is None else total + kept
    return total


def halo_lines(first, near_ref, far_ref, halo_ref, lines_ref):
    rows = slice(first * 144, first * 144 + far_ref.shape[0])
    lane = lax.broadcasted_iota(jnp.int32, far_ref.shape, 1)
    for half in range(2):
        low, high = near_ref[rows, :], far_ref[...]
        if half:
            low, high = high, low
        halo = jnp.concatenate(split(jnp.where(lane < 64, low, high)), axis=1)
        place = slice(half * 512, (half + 1) * 512)
        lines_ref[:, place] = jnp.dot(halo, halo_ref[:, place], preferred_element_type=F32)


def leave(i, source, source_at, state_out, sems):
    return [
        pltpu.make_async_copy(
            source.at[half, pl.ds(source_at * LEV, LEV)],
            state_out.at[pl.ds(ORDER[i] * LEV, LEV), pl.ds(8 * half, 8), :],
            sems.at[2 * i + half],
        )
        for half in range(2)
    ]


def into_halves(index, count, values, flat):
    for p, value in enumerate(values):
        flat[pl.ds(index * 64 + (p // 8) * (count * LEV * 8) + p % 8, 8, stride=8), :] = value


def third_kernel(owner_ref, code_ref, mark_ref, acc_ref, halo_ref, near_ref, far_ref,
                 mixed_ref, rain_ref,
                 lines_ref, dyn_ref, rain_rows, counts):
    halo_lines(0, near_ref, far_ref, halo_ref, lines_ref)
    turned = turned_edges(code_ref)
    flat = dyn_ref.reshape(2 * 3 * LEV * 8, LANES)
    flat_out = mixed_ref.reshape(2 * 3 * LEV * 8, LANES)

    def group(index, carry):
        into_halves(index, 3, averaged(index, index, turned, acc_ref, lines_ref), flat)
        return carry

    lax.fori_loop(0, 3 * GROUPS, group, 0)
    rain = physics(flat, mark_ref)
    for var in range(3):
        mixed(var, flat, flat_out)
    rain_rows[...] = by_span(rain) * (1.0 / LEV)
    rain_ref[...] = jnp.zeros_like(rain_ref)
    for owner in range(8):
        counts[owner] = 0
    for span in range(16):
        owner = owner_ref[span]
        rank = counts[owner]
        counts[owner] = rank + 1
        rain_ref[owner, pl.ds(rank, 1), :] = rain_rows[span : span + 1, :]


def fourth_kernel(code_ref, acc_hbm, halo_ref, near_ref, far_ref, mixed_ref, state_out,
                  lines_ref, acc_ref, dyn_ref, in_sems, sems):
    count = NVAR - 3
    held = [
        pltpu.make_async_copy(
            acc_hbm.at[pl.ds(i * ROWS, ROWS)], acc_ref.at[pl.ds(i * ROWS, ROWS)], in_sems.at[i]
        )
        for i in range(count)
    ]
    for copy in held:
        copy.start()
    halo_lines(3, near_ref, far_ref, halo_ref, lines_ref)
    turned = turned_edges(code_ref)
    flat = dyn_ref.reshape(2 * count * LEV * 8, LANES)

    def group(index, carry):
        into_halves(index, count, averaged(index, index, turned, acc_ref, lines_ref), flat)
        return carry

    copies = sum([leave(i, mixed_ref, i, state_out, sems) for i in range(3)], [])
    for copy in copies:
        copy.start()
    for i in range(count):
        held[i].wait()
        lax.fori_loop(i * GROUPS, (i + 1) * GROUPS, group, 0)
        for copy in leave(i + 3, dyn_ref, i, state_out, sems):
            copy.start()
            copies.append(copy)
    for copy in copies:
        copy.wait()


def swapped(value, axes, partner):
    count = lax.axis_size(axes)
    return lax.ppermute(value, axes, [(source, partner(source, count)) for source in range(count)])


def near_partner(source, count):
    return source + 1 if source % 2 == 0 else source - 1


def far_partner(source, count):
    return (source - 1) % count if source % 2 == 0 else (source + 1) % count


VM = pl.BlockSpec(memory_space=pltpu.VMEM)
SM = pl.BlockSpec(memory_space=pltpu.SMEM)
HB = pl.BlockSpec(memory_space=pltpu.HBM)


def shape(*sizes, dtype=F32):
    return jax.ShapeDtypeStruct(sizes, dtype)


def call(kernel, out, ins, outs, scratch, cost, **more):
    return pl.pallas_call(
        kernel,
        out_shape=out,
        in_specs=ins,
        out_specs=outs,
        scratch_shapes=scratch,
        cost_estimate=pl.CostEstimate(flops=cost, bytes_accessed=cost // 1000, transcendentals=0),
        compiler_params=pltpu.CompilerParams(vmem_limit_bytes=VMEM_LIMIT),
        **more,
    )


def in_hbm(value):
    return pltpu.with_memory_space_constraint(value, pltpu.HBM)


def body(state, metric, edge_peer, edge_code, span_owner, work_class):
    axes = ("elem", "col")
    devices = lax.axis_size(axes)
    state = state.reshape(NVAR * LEV, 16, LANES)
    metric = metric.reshape(32, LANES)
    owner = span_owner.reshape(16)
    count = NVAR - 3
    peer, code, work, slots, acc, high, low, near, far0, far1 = call(
        lambda *refs: first_kernel(devices, *refs),
        [
            shape(4, LANES, dtype=jnp.int32),
            shape(4, LANES, dtype=jnp.int32),
            shape(16, LANES, dtype=jnp.int32),
            shape(8, 512, dtype=jnp.int32),
            shape(NVAR * ROWS, LANES),
            shape(LINES, 1024, dtype=BF16),
            shape(LINES, 1024, dtype=BF16),
            shape(LINES, LANES),
            shape(3 * 144, LANES),
            shape(count * 144, LANES),
        ],
        [HB] * 5,
        [VM] * 10,
        [
            pltpu.VMEM((2, NVAR * LEV, 8, LANES), F32),
            pltpu.VMEM((32, LANES), F32),
            pltpu.VMEM((256, LANES), F32),
            pltpu.VMEM((512, 512), BF16),
            pltpu.VMEM((512, 512), BF16),
            pltpu.VMEM((256, 1024), BF16),
            pltpu.SemaphoreType.DMA((4,)),
            pltpu.SemaphoreType.DMA((NVAR, 2)),
        ],
        2_000_000_000,
    )(in_hbm(state), in_hbm(metric), in_hbm(edge_peer), in_hbm(edge_code), in_hbm(work_class))
    from_far0 = swapped(far0, axes, far_partner)
    from_near = swapped(near, axes, near_partner)
    from_far1 = swapped(far1, axes, far_partner)
    halo, acc, acc_rest = call(
        lambda *refs: second_kernel(devices, *refs),
        [shape(256, 1024, dtype=BF16), shape(3 * ROWS, LANES), shape(count * ROWS, LANES)],
        [VM] * 6,
        [VM] * 3,
        [
            pltpu.VMEM((512, 512), BF16),
            pltpu.VMEM((LINES, 1024), F32),
        ],
        4_000_000_000,
    )(peer, code, slots, acc, high, low)
    mixed1, rain = call(
        third_kernel,
        [shape(2, 3 * LEV, 8, LANES), shape(8, CAP, LANES)],
        [SM] + [VM] * 6,
        [VM, VM],
        [
            pltpu.VMEM((3 * 144, 1024), F32),
            pltpu.VMEM((2, 3 * LEV, 8, LANES), F32),
            pltpu.VMEM((16, LANES), F32),
            pltpu.SMEM((8,), jnp.int32),
        ],
        2_000_000_000,
    )(owner, code, work, acc, halo, from_near, from_far0)
    rain = lax.all_to_all(rain, "col", split_axis=0, concat_axis=0, tiled=True)
    new_state = call(
        fourth_kernel,
        shape(NVAR * LEV, 16, LANES),
        [VM, HB] + [VM] * 4,
        HB,
        [
            pltpu.VMEM((count * 144, 1024), F32),
            pltpu.VMEM((count * ROWS, LANES), F32),
            pltpu.VMEM((2, count * LEV, 8, LANES), F32),
            pltpu.SemaphoreType.DMA((count,)),
            pltpu.SemaphoreType.DMA((2 * NVAR,)),
        ],
        10_000_000_000,
    )(code, in_hbm(acc_rest), halo, from_near, from_far1, mixed1)
    new_state, rain = lax.optimization_barrier((new_state, rain))
    return new_state.reshape(NVAR, LEV, 16, LANES), rain.reshape(1, 1, 8 * CAP, LANES)


def solution(mesh):
    placed = (
        P(None, None, None, ("elem", "col")),
        P(None, None, ("elem", "col")),
        P(None, ("elem", "col")),
        P(None, ("elem", "col")),
        P(("elem", "col"), None),
        P(None, ("elem", "col")),
    )
    return jax.shard_map(
        body,
        mesh=mesh,
        in_specs=placed,
        out_specs=(P(None, None, None, ("elem", "col")), P("elem", "col", None, None)),
        check_vma=False,
    )
```

time: 38.6 us -> 35.3 us (0.915)
  local copies, waits for them, and re-layouts: 3.39 us -> 0.62 us
  starting transfers between devices: 17 us -> 15.4 us
  Pallas kernels: 15.6 us -> 16.6 us
    ppermute x2 -> x3, starting transfers between devices: 11.6 us -> 5.07 us  [swapped(): lax.ppermute(value, axes, [(source, partner(source, count)) for source in...]
    all_to_all x1, starting transfers between devices: 5.4 us -> 10.3 us  [body(): rain = lax.all_to_all(rain, 'col', split_axis=0, concat_axis=0, tiled=True)]
    unnamed x6 -> x4, local copies, waits for them, and re-layouts: 2.18 us -> 0.01 us
    pallas_call x3, Pallas kernels: 8.61 us -> 10.1 us  [the longest x1 3.5 us: body(): call(third_kernel, [shape(2, 3 * LEV, 8, LANES), shape(8, CAP, LANES)], [...]
    ppermute x2 -> x3, waiting for transfers between devices: 1.52 us -> 0.43 us  [swapped(): lax.ppermute(value, axes, [(source, partner(source, count)) for source in...]
    all_to_all x1, waiting for transfers between devices: 0.22 us -> 1.27 us  [body(): rain = lax.all_to_all(rain, 'col', split_axis=0, concat_axis=0, tiled=True)]
    reshape x1 -> x0, local copies, waits for them, and re-layouts: 0.6 us -> none  [body(): rain.reshape(8, CAP, LANES)]
    pallas_call x1, Pallas kernels: 6.97 us -> 6.58 us  [body(): call(lambda *refs: first_kernel(devices, *refs), [shape(4, LANES, dtype=j...]
  transfers between devices with their start and end apart: 3 -> 4, of which waited for: 2 -> 2; matrix products, arithmetic and copies ran while one was open for 0% -> 0% of each run, Pallas kernels for 14% -> 29%
where the time goes in v2:
time: 35.3 us; the launch traced here: 35 us
  Pallas kernels  16.6 us (47%)
  starting transfers between devices  15.4 us (44%)
  waiting for transfers between devices  1.71 us (5%)
  between operations  0.66 us (2%)
  local copies, waits for them, and re-layouts  0.62 us (2%)
    all_to_all x1, starting transfers between devices, body(): rain = lax.all_to_all(rain, 'col', split_axis=0, concat_axis=0, tiled=True)  10.3 us
    pallas_call x1, Pallas kernels, body(): call(lambda *refs: first_kernel(devices, *refs), [shape(4, LANES, dtype=j...  6.58 us
    ppermute x3, starting transfers between devices, swapped(): lax.ppermute(value, axes, [(source, partner(source, count)) for source in...  5.07 us
    pallas_call x1, Pallas kernels, body(): call(third_kernel, [shape(2, 3 * LEV, 8, LANES), shape(8, CAP, LANES)], [...  3.5 us
    pallas_call x1, Pallas kernels, body(): call(fourth_kernel, shape(NVAR * LEV, 16, LANES), [VM, HB] + [VM] * 4, HB...  3.39 us
    pallas_call x1, Pallas kernels, body(): call(lambda *refs: second_kernel(devices, *refs), [shape(256, 1024, dtype...  3.17 us
    all_to_all x1, waiting for transfers between devices, body(): rain = lax.all_to_all(rain, 'col', split_axis=0, concat_axis=0, tiled=True)  1.27 us
  transfers between devices with their start and end apart: 4, of which 2 were waited for; matrix products, arithmetic and copies ran while one was open for 0% of the time, Pallas kernels for 29%

profile of v2, /device:TPU:1, one launch (start us, length us, event | category | flops | bytes accessed | tf_op | source)
XLA Modules:
  0.0 35.0 jit_solution(400907586296517534)
XLA Ops:
  0.6 6.6 %shard_map.77 = (s32[4,128]{1,0:T(4,128)S(1)}, s32[4,128]{1,0:T(4,128)S(1)}, s32[16,128]{1,0:T(8,128)S(1)}, s32[8,512]{1,0:T(8,128)S(1)}, f32[8064,128]{1,0:T(8,...) custom-call(f32[504,16,128]{2,1,0:T(8,128)} %bitcast.5, ...), custom_call_target="tpu_custom_call" | custom-call | flops 2000000000 | bytes 2000000 | tf_op jit(solution)/shard_map/pallas_call | solution.py:514
  7.2 3.3 %collective-permute-start = (f32[1008,128]{1,0:T(8,128)S(1)}, f32[1008,128]{1,0:T(8,128)S(1)}, u32[]{:S(2)}, u32[]{:S(2)}) collective-permute-start(f32[1008,128]{1,0:T(8,128)S(1)} %get-tuple-element.27), channel_id=1, source_target_pairs={{0,1},{1,0},{2,3},{3,2},{4,5},{5,4},{6,7},{7,6},{8,9},{9,8},{10,11... | collective-permute-start | bytes 1548296 | tf_op jit(solution)/shard_map/ppermute | solution.py:470
  10.5 0.0 collective-permute-start.2
  10.5 1.7 %collective-permute-start.1 = (f32[576,128]{1,0:T(8,128)S(1)}, f32[576,128]{1,0:T(8,128)S(1)}, u32[]{:S(2)}, u32[]{:S(2)}) collective-permute-start(f32[576,128]{1,0:T(8,128)S(1)} %get-tuple-element.28), channel_id=1, source_target_pairs={{0,255},{1,2},{2,1},{3,4},{4,3},{5,6},{6,5},{7,8},{8,7},{9,10},{10... | collective-permute-start | bytes 884744 | tf_op jit(solution)/shard_map/ppermute | solution.py:470
  12.3 0.0 copy-start
  12.3 3.2 %shard_map.78 = (bf16[256,1024]{1,0:T(8,128)(2,1)S(1)}, f32[3456,128]{1,0:T(8,128)S(1)}, f32[4608,128]{1,0:T(8,128)S(1)}) custom-call(s32[4,128]{1,0:T(4,128)S(1)} %get-tuple-element.20.refs_0_, s32[4,128]{1,0:T(4,128)S(1)} %get-tuple-element.19.refs_1_.code_ref, s32[8,512]{1,0:T(8,128)S(1)} %get-tuple-element.21.refs_2_, ...), custom_call_target="tpu_custom_call" | custom-call | flops 4000000000 | bytes 4000000 | tf_op jit(solution)/shard_map/pallas_call | solution.py:545
  15.5 0.0 copy-start.1
  15.5 0.4 %collective-permute-done.2.far_ref = f32[432,128]{1,0:T(8,128)S(1)} collective-permute-done((f32[432,128]{1,0:T(8,128)S(1)}, f32[432,128]{1,0:T(8,128)S(1)}, u32[]{:S(2)}, u32[]{:S(2)}) %collective-permute-start.2) | collective-permute-done | bytes 221216 | tf_op jit(solution)/shard_map/ppermute | solution.py:470
  15.9 0.0 collective-permute-done.near_ref
  15.9 0.0 copy-done
  15.9 3.5 %shard_map.79 = (f32[2,216,8,128]{3,2,1,0:T(8,128)S(1)}, f32[8,3,128]{2,1,0:T(4,128)}) custom-call(s32[16]{0:T(128)S(1)} %bitcast.4, s32[4,128]{1,0:T(4,128)S(1)} %get-tuple-element.19.refs_1_.code_ref, s32[16,128]{1,0:T(8,128)S(1)} %get-tuple-element.29.mark_ref, f32[3456,128]{1,0:T(8,128)S(1)} %get-tuple-element.30.acc_ref, ...), custom_call_target="tpu_custom_call" | custom-call | flops 2000000000 | bytes 2000000 | tf_op jit(solution)/shard_map/pallas_call | solution.py:556
  19.4 0.0 copy-done.1
  19.4 10.3 %all-to-all-start = ((f32[8,3,128]{2,1,0:T(4,128)}), f32[8,3,128]{2,1,0:T(4,128)S(1)}, u32[]{:S(2)}, u32[]{:S(2)}) async-start(f32[8,3,128]{2,1,0:T(4,128)} %get-tuple-element.33), calls=%async_computation | async-start | bytes 32768 | tf_op jit(solution)/shard_map/all_to_all | solution.py:569
  29.8 0.0 collective-permute-done.1.far_ref
  29.8 3.4 %shard_map.80 = f32[504,16,128]{2,1,0:T(8,128)} custom-call(s32[4,128]{1,0:T(4,128)S(1)} %get-tuple-element.19.refs_1_.code_ref, f32[4608,128]{1,0:T(8,128)} %copy-done.1, bf16[256,1024]{1,0:T(8,128)(2,1)S(1)} %get-tuple-element.26.halo_ref, f32[1008,128]{1,0:T(8,128)S(1)} %collective-permute-done.near_ref, f32[576,128]{1,0:T(8,128)S(1)} %collective-permute-done.1.far_ref, ...), custom_call_target="tpu_custom_call" | custom-call | flops 10000000000 | bytes 10000000 | tf_op jit(solution)/shard_map/pallas_call | solution.py:570
  33.2 1.3 %all-to-all-done = f32[8,3,128]{2,1,0:T(4,128)S(1)} async-done(((f32[8,3,128]{2,1,0:T(4,128)}), f32[8,3,128]{2,1,0:T(4,128)S(1)}, u32[]{:S(2)}, u32[]{:S(2)}) %all-to-all-start) | async-done | bytes 12320 | tf_op jit(solution)/shard_map/all_to_all | solution.py:569
  34.4 0.6 %reshape.23 = f32[1,1,24,128]{3,2,1,0:T(8,128)} reshape(f32[8,3,128]{2,1,0:T(4,128)S(1)} %all-to-all-done) | data formatting | bytes 24576 | tf_op jit(solution)/shard_map/reshape | solution.py:585
Async XLA Ops:
  7.2 8.7 %collective-permute-start = (f32[1008,128]{1,0:T(8,128)S(1)}, f32[1008,128]{1,0:T(8,128)S(1)}, u32[]{:S(2)}, u32[]{:S(2)}) collective-permute-start(f32[1008,128]{1,0:T(8,128)S(1)} %get-tuple-element.27), channel_id=1, source_target_pairs={{0,1},{1,0},{2,3},{3,2},{4,5},{5,4},{6,7},{7,6},{8,9},{9,8},{10,11... | collective-permute-start | bytes 1548296 | tf_op jit(solution)/shard_map/ppermute | solution.py:470
  10.5 5.4 %collective-permute-start.2 = (f32[432,128]{1,0:T(8,128)S(1)}, f32[432,128]{1,0:T(8,128)S(1)}, u32[]{:S(2)}, u32[]{:S(2)}) collective-permute-start(f32[432,128]{1,0:T(8,128)S(1)} %get-tuple-element.31), channel_id=1, source_target_pairs={{0,255},{1,2},{2,1},{3,4},{4,3},{5,6},{6,5},{7,8},{8,7},{9,10},{10... | collective-permute-start | bytes 663560 | tf_op jit(solution)/shard_map/ppermute | solution.py:470
  10.5 19.2 %collective-permute-start.1 = (f32[576,128]{1,0:T(8,128)S(1)}, f32[576,128]{1,0:T(8,128)S(1)}, u32[]{:S(2)}, u32[]{:S(2)}) collective-permute-start(f32[576,128]{1,0:T(8,128)S(1)} %get-tuple-element.28), channel_id=1, source_target_pairs={{0,255},{1,2},{2,1},{3,4},{4,3},{5,6},{6,5},{7,8},{8,7},{9,10},{10... | collective-permute-start | bytes 884744 | tf_op jit(solution)/shard_map/ppermute | solution.py:470
  12.3 3.6 %copy-start = (s32[16,1]{0,1:T(1,128)S(1)}, s32[16,1]{0,1:T(1,128)}, u32[]{:S(2)}) copy-start(s32[16,1]{0,1:T(1,128)} %param.10) | copy-start | bytes 196
  15.5 4.0 %copy-start.1 = (f32[4608,128]{1,0:T(8,128)}, f32[4608,128]{1,0:T(8,128)S(1)}, u32[]{:S(2)}) copy-start(f32[4608,128]{1,0:T(8,128)S(1)} %get-tuple-element.25.acc_hbm) | copy-start | bytes 7077892
  19.4 15.0 %all-to-all-start = ((f32[8,3,128]{2,1,0:T(4,128)}), f32[8,3,128]{2,1,0:T(4,128)S(1)}, u32[]{:S(2)}, u32[]{:S(2)}) async-start(f32[8,3,128]{2,1,0:T(4,128)} %get-tuple-element.33), calls=%async_computation | async-start | bytes 32768 | tf_op jit(solution)/shard_map/all_to_all | solution.py:569

commit v3 on v2

--- a/solution.py
+++ b/solution.py
@@ -282,28 +282,28 @@
     return value
 
 
+def own_lines(first, count, high_ref, low_ref, own_ref, half):
+    rows = slice(first * 144, (first + count) * 144)
+    place = slice(half * 512, (half + 1) * 512)
+    return jnp.dot(high_ref[rows, place], own_ref[...], preferred_element_type=F32) + jnp.dot(
+        low_ref[rows, place], own_ref[...], preferred_element_type=F32
+    )
+
+
 def second_kernel(devices, peer_ref, code_ref, slots_ref, acc_ref, high_ref, low_ref,
-                  halo_ref, first_ref, rest_ref, own_ref, lines_ref):
+                  own_ref, halo_ref, first_ref, lines_ref):
     me = lax.axis_index(("elem", "col"))
     place_weights(edge_rows(peer_ref, code_ref, me, devices), slots_ref, own_ref, halo_ref)
-
     for half in range(2):
-        place = slice(half * 512, (half + 1) * 512)
-        lines_ref[:, place] = jnp.dot(
-            high_ref[:, place], own_ref[...], preferred_element_type=F32
-        ) + jnp.dot(low_ref[:, place], own_ref[...], preferred_element_type=F32)
+        lines_ref[:, half * 512 : (half + 1) * 512] = own_lines(0, 3, high_ref, low_ref, own_ref, half)
     turned = turned_edges(code_ref)
 
-    def group_into(out_ref, skipped):
-        def group(index, carry):
-            for p, value in enumerate(averaged(index, index, turned, acc_ref, lines_ref)):
-                out_ref[pl.ds(pl.multiple_of((index - skipped * GROUPS) * 128 + 8 * p, 8), 8), :] = value
-            return carry
-
-        return group
-
-    lax.fori_loop(0, 3 * GROUPS, group_into(first_ref, 0), 0)
-    lax.fori_loop(3 * GROUPS, NVAR * GROUPS, group_into(rest_ref, 3), 0)
+    def group(index, carry):
+        for p, value in enumerate(averaged(index, index, turned, acc_ref, lines_ref)):
+            first_ref[pl.ds(pl.multiple_of(index * 128 + 8 * p, 8), 8), :] = value
+        return carry
+
+    lax.fori_loop(0, 3 * GROUPS, group, 0)
 
 
 LOG2E = float(np.log2(np.e))
@@ -378,16 +378,14 @@
     return total
 
 
-def halo_lines(first, near_ref, far_ref, halo_ref, lines_ref):
+def halo_lines(first, near_ref, far_ref, halo_ref, half):
     rows = slice(first * 144, first * 144 + far_ref.shape[0])
     lane = lax.broadcasted_iota(jnp.int32, far_ref.shape, 1)
-    for half in range(2):
-        low, high = near_ref[rows, :], far_ref[...]
-        if half:
-            low, high = high, low
-        halo = jnp.concatenate(split(jnp.where(lane < 64, low, high)), axis=1)
-        place = slice(half * 512, (half + 1) * 512)
-        lines_ref[:, place] = jnp.dot(halo, halo_ref[:, place], preferred_element_type=F32)
+    low, high = near_ref[rows, :], far_ref[...]
+    if half:
+        low, high = high, low
+    halo = jnp.concatenate(split(jnp.where(lane < 64, low, high)), axis=1)
+    return jnp.dot(halo, halo_ref[:, half * 512 : (half + 1) * 512], preferred_element_type=F32)
 
 
 def leave(i, source, source_at, state_out, sems):
@@ -407,9 +405,11 @@
 
 
 def third_kernel(owner_ref, code_ref, mark_ref, acc_ref, halo_ref, near_ref, far_ref,
-                 mixed_ref, rain_ref,
+                 mixed_ref, keep_ref, send_ref,
                  lines_ref, dyn_ref, rain_rows, counts):
-    halo_lines(0, near_ref, far_ref, halo_ref, lines_ref)
+    me = lax.axis_index("col")
+    for half in range(2):
+        lines_ref[:, half * 512 : (half + 1) * 512] = halo_lines(0, near_ref, far_ref, halo_ref, half)
     turned = turned_edges(code_ref)
     flat = dyn_ref.reshape(2 * 3 * LEV * 8, LANES)
     flat_out = mixed_ref.reshape(2 * 3 * LEV * 8, LANES)
@@ -423,46 +423,59 @@
     for var in range(3):
         mixed(var, flat, flat_out)
     rain_rows[...] = by_span(rain) * (1.0 / LEV)
-    rain_ref[...] = jnp.zeros_like(rain_ref)
+    keep_ref[...] = jnp.zeros_like(keep_ref)
+    send_ref[...] = jnp.zeros_like(send_ref)
     for owner in range(8):
         counts[owner] = 0
     for span in range(16):
         owner = owner_ref[span]
         rank = counts[owner]
         counts[owner] = rank + 1
-        rain_ref[owner, pl.ds(rank, 1), :] = rain_rows[span : span + 1, :]
-
-
-def fourth_kernel(code_ref, acc_hbm, halo_ref, near_ref, far_ref, mixed_ref, state_out,
-                  lines_ref, acc_ref, dyn_ref, in_sems, sems):
+        way = lax.bitwise_xor(owner, me)
+        place = 8 * (way // 2 % 2) + 4 * (way // 4) + rank
+
+        @pl.when(way % 2 == 0)
+        def _(place=place, span=span):
+            keep_ref[pl.ds(place, 1), :] = rain_rows[span : span + 1, :]
+
+        @pl.when(way % 2 == 1)
+        def _(place=place, span=span):
+            send_ref[pl.ds(place, 1), :] = rain_rows[span : span + 1, :]
+
+
+def fourth_kernel(code_ref, acc_ref, high_ref, low_ref, own_ref, halo_ref, near_ref, far_ref,
+                  dyn_ref, lines_ref):
     count = NVAR - 3
-    held = [
-        pltpu.make_async_copy(
-            acc_hbm.at[pl.ds(i * ROWS, ROWS)], acc_ref.at[pl.ds(i * ROWS, ROWS)], in_sems.at[i]
-        )
-        for i in range(count)
-    ]
-    for copy in held:
-        copy.start()
-    halo_lines(3, near_ref, far_ref, halo_ref, lines_ref)
+    for half in range(2):
+        lines_ref[:, half * 512 : (half + 1) * 512] = own_lines(
+            3, count, high_ref, low_ref, own_ref, half
+        ) + halo_lines(3, near_ref, far_ref, halo_ref, half)
     turned = turned_edges(code_ref)
     flat = dyn_ref.reshape(2 * count * LEV * 8, LANES)
 
     def group(index, carry):
-        into_halves(index, count, averaged(index, index, turned, acc_ref, lines_ref), flat)
+        into_halves(index, count, averaged(index + 3 * GROUPS, index, turned, acc_ref, lines_ref), flat)
         return carry
 
+    lax.fori_loop(0, count * GROUPS, group, 0)
+
+
+def fifth_kernel(mixed_ref, dyn_ref, state_out, sems):
     copies = sum([leave(i, mixed_ref, i, state_out, sems) for i in range(3)], [])
+    copies += sum([leave(i + 3, dyn_ref, i, state_out, sems) for i in range(NVAR - 3)], [])
     for copy in copies:
         copy.start()
-    for i in range(count):
-        held[i].wait()
-        lax.fori_loop(i * GROUPS, (i + 1) * GROUPS, group, 0)
-        for copy in leave(i + 3, dyn_ref, i, state_out, sems):
-            copy.start()
-            copies.append(copy)
     for copy in copies:
         copy.wait()
+
+
+def sixth_kernel(keep_ref, first_ref, second_ref, third_ref, rain_ref):
+    me = lax.axis_index("col")
+    found = [keep_ref[0:4, :], first_ref[0:4, :], second_ref[0:4, :], second_ref[8:12, :]]
+    found += [third_ref[4 * i : 4 * i + 4, :] for i in range(4)]
+    for way, rows in enumerate(found):
+        for rank in range(CAP):
+            rain_ref[pl.ds(CAP * lax.bitwise_xor(me, way) + rank, 1), :] = rows[rank : rank + 1, :]
 
 
 def swapped(value, axes, partner):
@@ -542,22 +555,19 @@
     from_far0 = swapped(far0, axes, far_partner)
     from_near = swapped(near, axes, near_partner)
     from_far1 = swapped(far1, axes, far_partner)
-    halo, acc, acc_rest = call(
+    own, halo, first = call(
         lambda *refs: second_kernel(devices, *refs),
-        [shape(256, 1024, dtype=BF16), shape(3 * ROWS, LANES), shape(count * ROWS, LANES)],
+        [shape(512, 512, dtype=BF16), shape(256, 1024, dtype=BF16), shape(3 * ROWS, LANES)],
         [VM] * 6,
         [VM] * 3,
-        [
-            pltpu.VMEM((512, 512), BF16),
-            pltpu.VMEM((LINES, 1024), F32),
-        ],
-        4_000_000_000,
+        [pltpu.VMEM((3 * 144, 1024), F32)],
+        2_000_000_000,
     )(peer, code, slots, acc, high, low)
-    mixed1, rain = call(
+    mixed1, keep, send = call(
         third_kernel,
-        [shape(2, 3 * LEV, 8, LANES), shape(8, CAP, LANES)],
+        [shape(2, 3 * LEV, 8, LANES), shape(16, LANES), shape(16, LANES)],
         [SM] + [VM] * 6,
-        [VM, VM],
+        [VM] * 3,
         [
             pltpu.VMEM((3 * 144, 1024), F32),
             pltpu.VMEM((2, 3 * LEV, 8, LANES), F32),
@@ -565,23 +575,31 @@
             pltpu.SMEM((8,), jnp.int32),
         ],
         2_000_000_000,
-    )(owner, code, work, acc, halo, from_near, from_far0)
-    rain = lax.all_to_all(rain, "col", split_axis=0, concat_axis=0, tiled=True)
+    )(owner, code, work, first, halo, from_near, from_far0)
+    rain1 = swapped(send, "col", lambda source, size: source ^ 1)
+    dyn = call(
+        fourth_kernel,
+        shape(2, count * LEV, 8, LANES),
+        [VM] * 8,
+        VM,
+        [pltpu.VMEM((count * 144, 1024), F32)],
+        4_000_000_000,
+    )(code, acc, high, low, own, halo, from_near, from_far1)
+    keep, rain1, dyn = lax.optimization_barrier((keep, rain1, dyn))
+    send = jnp.concatenate([keep[8:16], rain1[8:16]], axis=0)
+    rain2 = swapped(send, "col", lambda source, size: source ^ 2)
     new_state = call(
-        fourth_kernel,
+        fifth_kernel,
         shape(NVAR * LEV, 16, LANES),
-        [VM, HB] + [VM] * 4,
+        [VM, VM],
         HB,
-        [
-            pltpu.VMEM((count * 144, 1024), F32),
-            pltpu.VMEM((count * ROWS, LANES), F32),
-            pltpu.VMEM((2, count * LEV, 8, LANES), F32),
-            pltpu.SemaphoreType.DMA((count,)),
-            pltpu.SemaphoreType.DMA((2 * NVAR,)),
-        ],
-        10_000_000_000,
-    )(code, in_hbm(acc_rest), halo, from_near, from_far1, mixed1)
-    new_state, rain = lax.optimization_barrier((new_state, rain))
+        [pltpu.SemaphoreType.DMA((2 * NVAR,))],
+        4_000_000_000,
+    )(mixed1, dyn)
+    keep, rain1, rain2, new_state = lax.optimization_barrier((keep, rain1, rain2, new_state))
+    send = jnp.concatenate([keep[4:8], rain1[4:8], rain2[4:8], rain2[12:16]], axis=0)
+    rain3 = swapped(send, "col", lambda source, size: source ^ 4)
+    rain = call(sixth_kernel, shape(8 * CAP, LANES), [VM] * 4, VM, [], 1_000_000)(keep, rain1, rain2, rain3)
     return new_state.reshape(NVAR, LEV, 16, LANES), rain.reshape(1, 1, 8 * CAP, LANES)
 
 

time: 35.3 us -> 40.6 us (1.15)
  the two profiles are of different devices: /device:TPU:1 before, /device:TPU:2 now
where the time goes in v3:
time: 40.6 us; the launch traced here: 40.5 us
  Pallas kernels  16.4 us (40%)
  starting transfers between devices  16.1 us (40%)
  waiting for transfers between devices  7.22 us (18%)
  between operations  0.76 us (2%)
    ppermute x6, starting transfers between devices, swapped(): lax.ppermute(value, axes, [(source, partner(source, count)) for source in...  16.1 us
    ppermute x6, waiting for transfers between devices, swapped(): lax.ppermute(value, axes, [(source, partner(source, count)) for source in...  7.22 us
    pallas_call x1, Pallas kernels, body(): call(lambda *refs: first_kernel(devices, *refs), [shape(4, LANES, dtype=j...  6.58 us
    pallas_call x1, Pallas kernels, body(): call(third_kernel, [shape(2, 3 * LEV, 8, LANES), shape(16, LANES), shape(...  3.32 us
    pallas_call x1, Pallas kernels, body(): call(fourth_kernel, shape(2, count * LEV, 8, LANES), [VM] * 8, VM, [pltpu...  2.3 us
    pallas_call x1, Pallas kernels, body(): call(fifth_kernel, shape(NVAR * LEV, 16, LANES), [VM, VM], HB, [pltpu.Sem...  2.1 us
    pallas_call x1, Pallas kernels, body(): call(lambda *refs: second_kernel(devices, *refs), [shape(512, 512, dtype=...  1.51 us
  transfers between devices with their start and end apart: 6, of which 2 were waited for; matrix products, arithmetic and copies ran while one was open for 0% of the time, Pallas kernels for 23%

profile of v3, /device:TPU:2, one launch (start us, length us, event | category | flops | bytes accessed | tf_op | source)
XLA Modules:
  0.0 40.5 jit_solution(3456516957009089181)
XLA Ops:
  0.6 6.6 %shard_map.77 = (s32[4,128]{1,0:T(4,128)S(1)}, s32[4,128]{1,0:T(4,128)S(1)}, s32[16,128]{1,0:T(8,128)S(1)}, s32[8,512]{1,0:T(8,128)S(1)}, f32[8064,128]{1,0:T(8,...) custom-call(f32[504,16,128]{2,1,0:T(8,128)} %bitcast.7, ...), custom_call_target="tpu_custom_call" | custom-call | flops 2000000000 | bytes 2000000 | tf_op jit(solution)/shard_map/pallas_call | solution.py:527
  7.2 0.1 collective-permute-start
  7.3 2.4 %collective-permute-start.1 = (f32[432,128]{1,0:T(8,128)S(1)}, f32[432,128]{1,0:T(8,128)S(1)}, u32[]{:S(2)}, u32[]{:S(2)}) collective-permute-start(f32[432,128]{1,0:T(8,128)S(1)} %get-tuple-element.35), channel_id=1, source_target_pairs={{0,255},{1,2},{2,1},{3,4},{4,3},{5,6},{6,5},{7,8},{8,7},{9,10},{10... | collective-permute-start | bytes 663560 | tf_op jit(solution)/shard_map/ppermute | solution.py:483
  9.7 0.0 collective-permute-start.3
  9.7 0.0 copy-start
  9.7 1.5 %shard_map.78 = (bf16[512,512]{1,0:T(8,128)(2,1)S(1)}, bf16[256,1024]{1,0:T(8,128)(2,1)S(1)}, f32[3456,128]{1,0:T(8,128)S(1)}) custom-call(s32[4,128]{1,0:T(4,128)S(1)} %get-tuple-element.27.refs_0_, s32[4,128]{1,0:T(4,128)S(1)} %get-tuple-element.25.refs_1_.code_ref, s32[8,512]{1,0:T(8,128)S(1)} %get-tuple-element.28.refs_2_, ...), custom_call_target="tpu_custom_call" | custom-call | flops 2000000000 | bytes 2000000 | tf_op jit(solution)/shard_map/pallas_call | solution.py:558
  11.2 2.1 %collective-permute-done.1.far_ref = f32[432,128]{1,0:T(8,128)S(1)} collective-permute-done((f32[432,128]{1,0:T(8,128)S(1)}, f32[432,128]{1,0:T(8,128)S(1)}, u32[]{:S(2)}, u32[]{:S(2)}) %collective-permute-start.1) | collective-permute-done | bytes 221216 | tf_op jit(solution)/shard_map/ppermute | solution.py:483
  13.3 0.0 collective-permute-done.near_ref
  13.3 0.0 copy-done
  13.3 3.3 %shard_map.79 = (f32[2,216,8,128]{3,2,1,0:T(8,128)S(1)}, f32[16,128]{1,0:T(8,128)S(1)}, f32[16,128]{1,0:T(8,128)S(1)}) custom-call(s32[16]{0:T(128)S(1)} %bitcast.5, s32[4,128]{1,0:T(4,128)S(1)} %get-tuple-element.25.refs_1_.code_ref, s32[16,128]{1,0:T(8,128)S(1)} %get-tuple-element.26.mark_ref, f32[3456,128]{1,0:T(8,128)S(1)} %get-tuple-element.32.acc_ref, ...), custom_call_target="tpu_custom_call" | custom-call | flops 2000000000 | bytes 2000000 | tf_op jit(solution)/shard_map/pallas_call | solution.py:566
  16.6 0.3 collective-permute-start.2
  16.9 0.0 collective-permute-done.3.far_ref
  16.9 2.3 %shard_map.80.dyn_ref = f32[2,288,8,128]{3,2,1,0:T(8,128)S(1)} custom-call(s32[4,128]{1,0:T(4,128)S(1)} %get-tuple-element.25.refs_1_.code_ref, f32[8064,128]{1,0:T(8,128)S(1)} %get-tuple-element.29.refs_3_.acc_ref, bf16[1008,1024]{1,0:T(8,128)(2,1)S(1)} %get-tuple-element.30.refs_4_.high_ref, bf16[1008,1024]{1,0:T(8,128)(2,1)S(1)} %get-tuple-element.31.refs_5_.low_ref, ...), custom_call_target="tpu_custom_call" | custom-call | flops 4000000000 | bytes 4000000 | tf_op jit(solution)/shard_map/pallas_call | solution.py:580
  19.2 0.0 collective-permute-done.2.first_ref
  19.2 13.2 %collective-permute-start.4 = (f32[16,128]{1,0:T(8,128)S(1)}, f32[16,128]{1,0:T(8,128)S(1)}, u32[]{:S(2)}, u32[]{:S(2)}) collective-permute-start(f32[16,128]{1,0:T(8,128)S(1)} %pad_maximum_fusion), channel_id=1, source_target_pairs={{0,2},{1,3},{2,0},{3,1},{4,6},{5,7},{6,4},{7,5},{8,10},{9,11},{10,... | collective-permute-start | bytes 24584 | tf_op jit(solution)/shard_map/ppermute | solution.py:483
  32.5 2.1 %shard_map.81 = f32[504,16,128]{2,1,0:T(8,128)} custom-call(f32[2,216,8,128]{3,2,1,0:T(8,128)S(1)} %get-tuple-element.42.mixed_ref, f32[2,288,8,128]{3,2,1,0:T(8,128)S(1)} %shard_map.80.dyn_ref), custom_call_target="tpu_custom_call" | custom-call | flops 4000000000 | bytes 4000000 | tf_op jit(solution)/shard_map/pallas_call | solution.py:591
  34.6 0.0 collective-permute-done.4.second_ref
  34.6 0.1 collective-permute-start.5
  34.7 5.1 %collective-permute-done.5.third_ref = f32[16,128]{1,0:T(8,128)S(1)} collective-permute-done((f32[16,128]{1,0:T(8,128)S(1)}, f32[16,128]{1,0:T(8,128)S(1)}, u32[]{:S(2)}, u32[]{:S(2)}) %collective-permute-start.5) | collective-permute-done | bytes 8224 | tf_op jit(solution)/shard_map/ppermute | solution.py:483
  39.9 0.6 %shard_map.82 = f32[24,128]{1,0:T(8,128)} custom-call(f32[16,128]{1,0:T(8,128)S(1)} %get-tuple-element.45.keep_ref, f32[16,128]{1,0:T(8,128)S(1)} %collective-permute-done.2.first_ref, f32[16,128]{1,0:T(8,128)S(1)} %collective-permute-done.4.second_ref, f32[16,128]{1,0:T(8,128)S(1)} %collective-permute-done.5.third_ref), custom_call_target="tpu_custom_call" | custom-call | flops 1000000 | bytes 1000 | tf_op jit(solution)/shard_map/pallas_call | solution.py:602
  (7 shorter events, 0.0 us)
Async XLA Ops:
  7.2 6.1 %collective-permute-start = (f32[1008,128]{1,0:T(8,128)S(1)}, f32[1008,128]{1,0:T(8,128)S(1)}, u32[]{:S(2)}, u32[]{:S(2)}) collective-permute-start(f32[1008,128]{1,0:T(8,128)S(1)} %get-tuple-element.34), channel_id=1, source_target_pairs={{0,1},{1,0},{2,3},{3,2},{4,5},{5,4},{6,7},{7,6},{8,9},{9,8},{10,11... | collective-permute-start | bytes 1548296 | tf_op jit(solution)/shard_map/ppermute | solution.py:483
  7.3 6.0 %collective-permute-start.1 = (f32[432,128]{1,0:T(8,128)S(1)}, f32[432,128]{1,0:T(8,128)S(1)}, u32[]{:S(2)}, u32[]{:S(2)}) collective-permute-start(f32[432,128]{1,0:T(8,128)S(1)} %get-tuple-element.35), channel_id=1, source_target_pairs={{0,255},{1,2},{2,1},{3,4},{4,3},{5,6},{6,5},{7,8},{8,7},{9,10},{10... | collective-permute-start | bytes 663560 | tf_op jit(solution)/shard_map/ppermute | solution.py:483
  9.7 7.2 %collective-permute-start.3 = (f32[576,128]{1,0:T(8,128)S(1)}, f32[576,128]{1,0:T(8,128)S(1)}, u32[]{:S(2)}, u32[]{:S(2)}) collective-permute-start(f32[576,128]{1,0:T(8,128)S(1)} %get-tuple-element.39), channel_id=1, source_target_pairs={{0,255},{1,2},{2,1},{3,4},{4,3},{5,6},{6,5},{7,8},{8,7},{9,10},{10... | collective-permute-start | bytes 884744 | tf_op jit(solution)/shard_map/ppermute | solution.py:483
  9.7 3.6 %copy-start = (s32[16,1]{0,1:T(1,128)S(1)}, s32[16,1]{0,1:T(1,128)}, u32[]{:S(2)}) copy-start(s32[16,1]{0,1:T(1,128)} %param.10) | copy-start | bytes 196
  16.6 2.6 %collective-permute-start.2 = (f32[16,128]{1,0:T(8,128)S(1)}, f32[16,128]{1,0:T(8,128)S(1)}, u32[]{:S(2)}, u32[]{:S(2)}) collective-permute-start(f32[16,128]{1,0:T(8,128)S(1)} %get-tuple-element.37), channel_id=1, source_target_pairs={{0,1},{1,0},{2,3},{3,2},{4,5},{5,4},{6,7},{7,6},{8,9},{9,8},{10,11... | collective-permute-start | bytes 24584 | tf_op jit(solution)/shard_map/ppermute | solution.py:483
  19.2 15.3 %collective-permute-start.4 = (f32[16,128]{1,0:T(8,128)S(1)}, f32[16,128]{1,0:T(8,128)S(1)}, u32[]{:S(2)}, u32[]{:S(2)}) collective-permute-start(f32[16,128]{1,0:T(8,128)S(1)} %pad_maximum_fusion), channel_id=1, source_target_pairs={{0,2},{1,3},{2,0},{3,1},{4,6},{5,7},{6,4},{7,5},{8,10},{9,11},{10,... | collective-permute-start | bytes 24584 | tf_op jit(solution)/shard_map/ppermute | solution.py:483
  34.6 5.2 %collective-permute-start.5 = (f32[16,128]{1,0:T(8,128)S(1)}, f32[16,128]{1,0:T(8,128)S(1)}, u32[]{:S(2)}, u32[]{:S(2)}) collective-permute-start(f32[16,128]{1,0:T(8,128)S(1)} %pad_maximum_fusion.1), channel_id=1, source_target_pairs={{0,4},{1,5},{2,6},{3,7},{4,0},{5,1},{6,2},{7,3},{8,12},{9,13},{10,... | collective-permute-start | bytes 24584 | tf_op jit(solution)/shard_map/ppermute | solution.py:483

commit v4 on v2

--- a/solution.py
+++ b/solution.py
@@ -16,7 +16,7 @@
 SCALE = 0.5 * 0.03
 ORDER = (2, 3, 4, 0, 1, 5, 6)
 NVAR = 7
-AHEAD = 3
+AHEAD = 2
 LINES = NVAR * GROUPS * 16
 CAP = 3
 F32 = jnp.float32
@@ -196,7 +196,12 @@
 
     def variable(var, carry):
         ready(var)
-        return lax.fori_loop(var * GROUPS, (var + 1) * GROUPS, group, carry)
+        def three(index, carry):
+            for i in range(3):
+                group(var * GROUPS + 3 * index + i, carry)
+            return carry
+
+        return lax.fori_loop(0, GROUPS // 3, three, carry)
 
     lax.fori_loop(0, NVAR, variable, 0)
     across = (((1,), (1,)), ((), ()))
@@ -302,8 +307,8 @@
 
         return group
 
-    lax.fori_loop(0, 3 * GROUPS, group_into(first_ref, 0), 0)
-    lax.fori_loop(3 * GROUPS, NVAR * GROUPS, group_into(rest_ref, 3), 0)
+    lax.fori_loop(0, 3 * GROUPS, group_into(first_ref, 0), 0, unroll=3)
+    lax.fori_loop(3 * GROUPS, NVAR * GROUPS, group_into(rest_ref, 3), 0, unroll=3)
 
 
 LOG2E = float(np.log2(np.e))
@@ -418,7 +423,7 @@
         into_halves(index, 3, averaged(index, index, turned, acc_ref, lines_ref), flat)
         return carry
 
-    lax.fori_loop(0, 3 * GROUPS, group, 0)
+    lax.fori_loop(0, 3 * GROUPS, group, 0, unroll=3)
     rain = physics(flat, mark_ref)
     for var in range(3):
         mixed(var, flat, flat_out)
@@ -457,7 +462,7 @@
         copy.start()
     for i in range(count):
         held[i].wait()
-        lax.fori_loop(i * GROUPS, (i + 1) * GROUPS, group, 0)
+        lax.fori_loop(i * GROUPS, (i + 1) * GROUPS, group, 0, unroll=3)
         for copy in leave(i + 3, dyn_ref, i, state_out, sems):
             copy.start()
             copies.append(copy)

time: 35.3 us -> 35.2 us (level)
  transfers between devices with their start and end apart: 4 -> 4, of which waited for: 2 -> 2; matrix products, arithmetic and copies ran while one was open for 0% -> 0% of each run, Pallas kernels for 29% -> 28%
where the time goes in v4:
time: 35.2 us; the launch traced here: 34.9 us
  Pallas kernels  16.4 us (47%)
  starting transfers between devices  15.4 us (44%)
  waiting for transfers between devices  1.81 us (5%)
  between operations  0.67 us (2%)
  local copies, waits for them, and re-layouts  0.62 us (2%)
    all_to_all x1, starting transfers between devices, body(): rain = lax.all_to_all(rain, 'col', split_axis=0, concat_axis=0, tiled=True)  10.3 us
    pallas_call x1, Pallas kernels, body(): call(lambda *refs: first_kernel(devices, *refs), [shape(4, LANES, dtype=j...  6.53 us
    ppermute x3, starting transfers between devices, swapped(): lax.ppermute(value, axes, [(source, partner(source, count)) for source in...  5.06 us
    pallas_call x1, Pallas kernels, body(): call(third_kernel, [shape(2, 3 * LEV, 8, LANES), shape(8, CAP, LANES)], [...  3.45 us
    pallas_call x1, Pallas kernels, body(): call(fourth_kernel, shape(NVAR * LEV, 16, LANES), [VM, HB] + [VM] * 4, HB...  3.36 us
    pallas_call x1, Pallas kernels, body(): call(lambda *refs: second_kernel(devices, *refs), [shape(256, 1024, dtype...  3.09 us
    all_to_all x1, waiting for transfers between devices, body(): rain = lax.all_to_all(rain, 'col', split_axis=0, concat_axis=0, tiled=True)  1.3 us
  transfers between devices with their start and end apart: 4, of which 2 were waited for; matrix products, arithmetic and copies ran while one was open for 0% of the time, Pallas kernels for 28%

profile of v4, /device:TPU:1, one launch (start us, length us, event | category | flops | bytes accessed | tf_op | source)
XLA Modules:
  0.0 34.9 jit_solution(17597726731197310640)
XLA Ops:
  0.6 6.5 %shard_map.77 = (s32[4,128]{1,0:T(4,128)S(1)}, s32[4,128]{1,0:T(4,128)S(1)}, s32[16,128]{1,0:T(8,128)S(1)}, s32[8,512]{1,0:T(8,128)S(1)}, f32[8064,128]{1,0:T(8,...) custom-call(f32[504,16,128]{2,1,0:T(8,128)} %bitcast.5, ...), custom_call_target="tpu_custom_call" | custom-call | flops 2000000000 | bytes 2000000 | tf_op jit(solution)/shard_map/pallas_call | solution.py:519
  7.2 3.3 %collective-permute-start = (f32[1008,128]{1,0:T(8,128)S(1)}, f32[1008,128]{1,0:T(8,128)S(1)}, u32[]{:S(2)}, u32[]{:S(2)}) collective-permute-start(f32[1008,128]{1,0:T(8,128)S(1)} %get-tuple-element.27), channel_id=1, source_target_pairs={{0,1},{1,0},{2,3},{3,2},{4,5},{5,4},{6,7},{7,6},{8,9},{9,8},{10,11... | collective-permute-start | bytes 1548296 | tf_op jit(solution)/shard_map/ppermute | solution.py:475
  10.5 0.0 collective-permute-start.2
  10.5 1.7 %collective-permute-start.1 = (f32[576,128]{1,0:T(8,128)S(1)}, f32[576,128]{1,0:T(8,128)S(1)}, u32[]{:S(2)}, u32[]{:S(2)}) collective-permute-start(f32[576,128]{1,0:T(8,128)S(1)} %get-tuple-element.28), channel_id=1, source_target_pairs={{0,255},{1,2},{2,1},{3,4},{4,3},{5,6},{6,5},{7,8},{8,7},{9,10},{10... | collective-permute-start | bytes 884744 | tf_op jit(solution)/shard_map/ppermute | solution.py:475
  12.2 0.0 copy-start
  12.2 3.1 %shard_map.78 = (bf16[256,1024]{1,0:T(8,128)(2,1)S(1)}, f32[3456,128]{1,0:T(8,128)S(1)}, f32[4608,128]{1,0:T(8,128)S(1)}) custom-call(s32[4,128]{1,0:T(4,128)S(1)} %get-tuple-element.20.refs_0_, s32[4,128]{1,0:T(4,128)S(1)} %get-tuple-element.19.refs_1_.code_ref, s32[8,512]{1,0:T(8,128)S(1)} %get-tuple-element.21.refs_2_, ...), custom_call_target="tpu_custom_call" | custom-call | flops 4000000000 | bytes 4000000 | tf_op jit(solution)/shard_map/pallas_call | solution.py:550
  15.3 0.0 copy-start.1
  15.3 0.5 %collective-permute-done.2.far_ref = f32[432,128]{1,0:T(8,128)S(1)} collective-permute-done((f32[432,128]{1,0:T(8,128)S(1)}, f32[432,128]{1,0:T(8,128)S(1)}, u32[]{:S(2)}, u32[]{:S(2)}) %collective-permute-start.2) | collective-permute-done | bytes 221216 | tf_op jit(solution)/shard_map/ppermute | solution.py:475
  15.8 0.0 collective-permute-done.near_ref
  15.9 0.0 copy-done
  15.9 3.5 %shard_map.79 = (f32[2,216,8,128]{3,2,1,0:T(8,128)S(1)}, f32[8,3,128]{2,1,0:T(4,128)}) custom-call(s32[16]{0:T(128)S(1)} %bitcast.4, s32[4,128]{1,0:T(4,128)S(1)} %get-tuple-element.19.refs_1_.code_ref, s32[16,128]{1,0:T(8,128)S(1)} %get-tuple-element.29.mark_ref, f32[3456,128]{1,0:T(8,128)S(1)} %get-tuple-element.30.acc_ref, ...), custom_call_target="tpu_custom_call" | custom-call | flops 2000000000 | bytes 2000000 | tf_op jit(solution)/shard_map/pallas_call | solution.py:561
  19.3 0.0 copy-done.1
  19.3 10.3 %all-to-all-start = ((f32[8,3,128]{2,1,0:T(4,128)}), f32[8,3,128]{2,1,0:T(4,128)S(1)}, u32[]{:S(2)}, u32[]{:S(2)}) async-start(f32[8,3,128]{2,1,0:T(4,128)} %get-tuple-element.33), calls=%async_computation | async-start | bytes 32768 | tf_op jit(solution)/shard_map/all_to_all | solution.py:574
  29.7 0.0 collective-permute-done.1.far_ref
  29.7 3.4 %shard_map.80 = f32[504,16,128]{2,1,0:T(8,128)} custom-call(s32[4,128]{1,0:T(4,128)S(1)} %get-tuple-element.19.refs_1_.code_ref, f32[4608,128]{1,0:T(8,128)} %copy-done.1, bf16[256,1024]{1,0:T(8,128)(2,1)S(1)} %get-tuple-element.26.halo_ref, f32[1008,128]{1,0:T(8,128)S(1)} %collective-permute-done.near_ref, f32[576,128]{1,0:T(8,128)S(1)} %collective-permute-done.1.far_ref, ...), custom_call_target="tpu_custom_call" | custom-call | flops 10000000000 | bytes 10000000 | tf_op jit(solution)/shard_map/pallas_call | solution.py:575
  33.0 1.3 %all-to-all-done = f32[8,3,128]{2,1,0:T(4,128)S(1)} async-done(((f32[8,3,128]{2,1,0:T(4,128)}), f32[8,3,128]{2,1,0:T(4,128)S(1)}, u32[]{:S(2)}, u32[]{:S(2)}) %all-to-all-start) | async-done | bytes 12320 | tf_op jit(solution)/shard_map/all_to_all | solution.py:574
  34.3 0.6 %reshape.23 = f32[1,1,24,128]{3,2,1,0:T(8,128)} reshape(f32[8,3,128]{2,1,0:T(4,128)S(1)} %all-to-all-done) | data formatting | bytes 24576 | tf_op jit(solution)/shard_map/reshape | solution.py:590
Async XLA Ops:
  7.2 8.7 %collective-permute-start = (f32[1008,128]{1,0:T(8,128)S(1)}, f32[1008,128]{1,0:T(8,128)S(1)}, u32[]{:S(2)}, u32[]{:S(2)}) collective-permute-start(f32[1008,128]{1,0:T(8,128)S(1)} %get-tuple-element.27), channel_id=1, source_target_pairs={{0,1},{1,0},{2,3},{3,2},{4,5},{5,4},{6,7},{7,6},{8,9},{9,8},{10,11... | collective-permute-start | bytes 1548296 | tf_op jit(solution)/shard_map/ppermute | solution.py:475
  10.5 5.4 %collective-permute-start.2 = (f32[432,128]{1,0:T(8,128)S(1)}, f32[432,128]{1,0:T(8,128)S(1)}, u32[]{:S(2)}, u32[]{:S(2)}) collective-permute-start(f32[432,128]{1,0:T(8,128)S(1)} %get-tuple-element.31), channel_id=1, source_target_pairs={{0,255},{1,2},{2,1},{3,4},{4,3},{5,6},{6,5},{7,8},{8,7},{9,10},{10... | collective-permute-start | bytes 663560 | tf_op jit(solution)/shard_map/ppermute | solution.py:475
  10.5 19.2 %collective-permute-start.1 = (f32[576,128]{1,0:T(8,128)S(1)}, f32[576,128]{1,0:T(8,128)S(1)}, u32[]{:S(2)}, u32[]{:S(2)}) collective-permute-start(f32[576,128]{1,0:T(8,128)S(1)} %get-tuple-element.28), channel_id=1, source_target_pairs={{0,255},{1,2},{2,1},{3,4},{4,3},{5,6},{6,5},{7,8},{8,7},{9,10},{10... | collective-permute-start | bytes 884744 | tf_op jit(solution)/shard_map/ppermute | solution.py:475
  12.2 3.6 %copy-start = (s32[16,1]{0,1:T(1,128)S(1)}, s32[16,1]{0,1:T(1,128)}, u32[]{:S(2)}) copy-start(s32[16,1]{0,1:T(1,128)} %param.10) | copy-start | bytes 196
  15.3 4.0 %copy-start.1 = (f32[4608,128]{1,0:T(8,128)}, f32[4608,128]{1,0:T(8,128)S(1)}, u32[]{:S(2)}) copy-start(f32[4608,128]{1,0:T(8,128)S(1)} %get-tuple-element.25.acc_hbm) | copy-start | bytes 7077892
  19.3 15.0 %all-to-all-start = ((f32[8,3,128]{2,1,0:T(4,128)}), f32[8,3,128]{2,1,0:T(4,128)S(1)}, u32[]{:S(2)}, u32[]{:S(2)}) async-start(f32[8,3,128]{2,1,0:T(4,128)} %get-tuple-element.33), calls=%async_computation | async-start | bytes 32768 | tf_op jit(solution)/shard_map/all_to_all | solution.py:574

commit v5 on v4

--- a/solution.py
+++ b/solution.py
@@ -109,18 +109,21 @@
 
 
 def slots_of(rows, even, hit_ref, less_ref, pack_ref, slots_ref):
-    number = lax.broadcasted_iota(jnp.int32, (512, LANES), 0)
+    number = lax.broadcasted_iota(jnp.int32, (LANES, LANES), 0)
+    line = lax.broadcasted_iota(jnp.int32, (16, LANES), 0)
     for k, row in enumerate(rows):
         low = slice(k * LANES, (k + 1) * LANES)
-        hit_ref[:, low] = one_hot(number == jnp.where(row["before"], row["source"], -1))
-        less_ref[:, low] = one_hot(number < row["source"])
+        hit_ref[:, low] = one_hot((line == lax.shift_right_logical(row["source"], 7)) & row["before"])
+        less_ref[:, low] = one_hot(number == lax.bitwise_and(row["source"], LANES - 1))
     met = lax.dot_general(
-        jnp.ones((16, 512), BF16), hit_ref[...], (((1,), (1,)), ((), ())), preferred_element_type=F32
+        hit_ref[...], less_ref[...], (((1,), (1,)), ((), ())), preferred_element_type=F32
     )
-    before_slot = jnp.dot(met.astype(BF16), less_ref[...], preferred_element_type=F32)
-    lower = one_hot(
-        lax.broadcasted_iota(jnp.int32, (LANES, LANES), 0) < lax.broadcasted_iota(jnp.int32, (LANES, LANES), 1)
-    )
+    lower = one_hot(number < lax.broadcasted_iota(jnp.int32, (LANES, LANES), 1))
+    sums = jnp.sum(met, axis=1, keepdims=True)
+    counted = jnp.dot(met.astype(BF16), lower, preferred_element_type=F32)
+    for k in range(3):
+        counted = counted + jnp.where(line > k, sums[k : k + 1, :], 0.0)
+    sent = jnp.dot(counted.astype(BF16), less_ref[...], preferred_element_type=F32)
     passed = jnp.zeros((1, 1), F32)
     slot = lax.broadcasted_iota(jnp.int32, (64, LANES), 0)
     for k, row in enumerate(rows):
@@ -131,7 +134,9 @@
         )
         passed = passed + jnp.sum(meets, axis=1, keepdims=True)
         after = jnp.where(row["after"], after_slot[0:1, :], -1.0).astype(jnp.int32)
-        before = jnp.where(row["before"], before_slot[0:1, low], -1.0).astype(jnp.int32)
+        own_line = line == lax.shift_right_logical(row["source"], 7)
+        before_slot = jnp.sum(jnp.where(own_line, sent[:, low], 0.0), axis=0, keepdims=True)
+        before = jnp.where(row["before"], before_slot, -1.0).astype(jnp.int32)
         near = jnp.where(even, after, before)
         far = jnp.where(even, before, after)
         slots_ref[0:1, low] = near
@@ -536,8 +541,8 @@
             pltpu.VMEM((2, NVAR * LEV, 8, LANES), F32),
             pltpu.VMEM((32, LANES), F32),
             pltpu.VMEM((256, LANES), F32),
-            pltpu.VMEM((512, 512), BF16),
-            pltpu.VMEM((512, 512), BF16),
+            pltpu.VMEM((16, 512), BF16),
+            pltpu.VMEM((LANES, 512), BF16),
             pltpu.VMEM((256, 1024), BF16),
             pltpu.SemaphoreType.DMA((4,)),
             pltpu.SemaphoreType.DMA((NVAR, 2)),

time: 35.2 us -> 35.2 us (level)
  no operation moved by 1% of the time
where the time goes in v5:
time: 35.2 us; the launch traced here: 35 us
  Pallas kernels  16.4 us (47%)
  starting transfers between devices  15.4 us (44%)
  waiting for transfers between devices  1.81 us (5%)
  between operations  0.67 us (2%)
  local copies, waits for them, and re-layouts  0.62 us (2%)
    all_to_all x1, starting transfers between devices, body(): rain = lax.all_to_all(rain, 'col', split_axis=0, concat_axis=0, tiled=True)  10.4 us
    pallas_call x1, Pallas kernels, body(): call(lambda *refs: first_kernel(devices, *refs), [shape(4, LANES, dtype=j...  6.54 us
    ppermute x3, starting transfers between devices, swapped(): lax.ppermute(value, axes, [(source, partner(source, count)) for source in...  5.07 us
    pallas_call x1, Pallas kernels, body(): call(third_kernel, [shape(2, 3 * LEV, 8, LANES), shape(8, CAP, LANES)], [...  3.45 us
    pallas_call x1, Pallas kernels, body(): call(fourth_kernel, shape(NVAR * LEV, 16, LANES), [VM, HB] + [VM] * 4, HB...  3.36 us
    pallas_call x1, Pallas kernels, body(): call(lambda *refs: second_kernel(devices, *refs), [shape(256, 1024, dtype...  3.09 us
    all_to_all x1, waiting for transfers between devices, body(): rain = lax.all_to_all(rain, 'col', split_axis=0, concat_axis=0, tiled=True)  1.3 us
  transfers between devices with their start and end apart: 4, of which 2 were waited for; matrix products, arithmetic and copies ran while one was open for 0% of the time, Pallas kernels for 28%

profile of v5, /device:TPU:1, one launch (start us, length us, event | category | flops | bytes accessed | tf_op | source)
XLA Modules:
  0.0 35.0 jit_solution(18396303699189205795)
XLA Ops:
  0.6 6.5 %shard_map.77 = (s32[4,128]{1,0:T(4,128)S(1)}, s32[4,128]{1,0:T(4,128)S(1)}, s32[16,128]{1,0:T(8,128)S(1)}, s32[8,512]{1,0:T(8,128)S(1)}, f32[8064,128]{1,0:T(8,...) custom-call(f32[504,16,128]{2,1,0:T(8,128)} %bitcast.5, ...), custom_call_target="tpu_custom_call" | custom-call | flops 2000000000 | bytes 2000000 | tf_op jit(solution)/shard_map/pallas_call | solution.py:524
  7.2 3.3 %collective-permute-start = (f32[1008,128]{1,0:T(8,128)S(1)}, f32[1008,128]{1,0:T(8,128)S(1)}, u32[]{:S(2)}, u32[]{:S(2)}) collective-permute-start(f32[1008,128]{1,0:T(8,128)S(1)} %get-tuple-element.27), channel_id=1, source_target_pairs={{0,1},{1,0},{2,3},{3,2},{4,5},{5,4},{6,7},{7,6},{8,9},{9,8},{10,11... | collective-permute-start | bytes 1548296 | tf_op jit(solution)/shard_map/ppermute | solution.py:480
  10.5 0.0 collective-permute-start.2
  10.5 1.7 %collective-permute-start.1 = (f32[576,128]{1,0:T(8,128)S(1)}, f32[576,128]{1,0:T(8,128)S(1)}, u32[]{:S(2)}, u32[]{:S(2)}) collective-permute-start(f32[576,128]{1,0:T(8,128)S(1)} %get-tuple-element.28), channel_id=1, source_target_pairs={{0,255},{1,2},{2,1},{3,4},{4,3},{5,6},{6,5},{7,8},{8,7},{9,10},{10... | collective-permute-start | bytes 884744 | tf_op jit(solution)/shard_map/ppermute | solution.py:480
  12.2 0.0 copy-start
  12.3 3.1 %shard_map.78 = (bf16[256,1024]{1,0:T(8,128)(2,1)S(1)}, f32[3456,128]{1,0:T(8,128)S(1)}, f32[4608,128]{1,0:T(8,128)S(1)}) custom-call(s32[4,128]{1,0:T(4,128)S(1)} %get-tuple-element.20.refs_0_, s32[4,128]{1,0:T(4,128)S(1)} %get-tuple-element.19.refs_1_.code_ref, s32[8,512]{1,0:T(8,128)S(1)} %get-tuple-element.21.refs_2_, ...), custom_call_target="tpu_custom_call" | custom-call | flops 4000000000 | bytes 4000000 | tf_op jit(solution)/shard_map/pallas_call | solution.py:555
  15.4 0.0 copy-start.1
  15.4 0.5 %collective-permute-done.2.far_ref = f32[432,128]{1,0:T(8,128)S(1)} collective-permute-done((f32[432,128]{1,0:T(8,128)S(1)}, f32[432,128]{1,0:T(8,128)S(1)}, u32[]{:S(2)}, u32[]{:S(2)}) %collective-permute-start.2) | collective-permute-done | bytes 221216 | tf_op jit(solution)/shard_map/ppermute | solution.py:480
  15.9 0.0 collective-permute-done.near_ref
  15.9 0.0 copy-done
  15.9 3.5 %shard_map.79 = (f32[2,216,8,128]{3,2,1,0:T(8,128)S(1)}, f32[8,3,128]{2,1,0:T(4,128)}) custom-call(s32[16]{0:T(128)S(1)} %bitcast.4, s32[4,128]{1,0:T(4,128)S(1)} %get-tuple-element.19.refs_1_.code_ref, s32[16,128]{1,0:T(8,128)S(1)} %get-tuple-element.29.mark_ref, f32[3456,128]{1,0:T(8,128)S(1)} %get-tuple-element.30.acc_ref, ...), custom_call_target="tpu_custom_call" | custom-call | flops 2000000000 | bytes 2000000 | tf_op jit(solution)/shard_map/pallas_call | solution.py:566
  19.3 0.0 copy-done.1
  19.3 10.4 %all-to-all-start = ((f32[8,3,128]{2,1,0:T(4,128)}), f32[8,3,128]{2,1,0:T(4,128)S(1)}, u32[]{:S(2)}, u32[]{:S(2)}) async-start(f32[8,3,128]{2,1,0:T(4,128)} %get-tuple-element.33), calls=%async_computation | async-start | bytes 32768 | tf_op jit(solution)/shard_map/all_to_all | solution.py:579
  29.7 0.0 collective-permute-done.1.far_ref
  29.7 3.4 %shard_map.80 = f32[504,16,128]{2,1,0:T(8,128)} custom-call(s32[4,128]{1,0:T(4,128)S(1)} %get-tuple-element.19.refs_1_.code_ref, f32[4608,128]{1,0:T(8,128)} %copy-done.1, bf16[256,1024]{1,0:T(8,128)(2,1)S(1)} %get-tuple-element.26.halo_ref, f32[1008,128]{1,0:T(8,128)S(1)} %collective-permute-done.near_ref, f32[576,128]{1,0:T(8,128)S(1)} %collective-permute-done.1.far_ref, ...), custom_call_target="tpu_custom_call" | custom-call | flops 10000000000 | bytes 10000000 | tf_op jit(solution)/shard_map/pallas_call | solution.py:580
  33.0 1.3 %all-to-all-done = f32[8,3,128]{2,1,0:T(4,128)S(1)} async-done(((f32[8,3,128]{2,1,0:T(4,128)}), f32[8,3,128]{2,1,0:T(4,128)S(1)}, u32[]{:S(2)}, u32[]{:S(2)}) %all-to-all-start) | async-done | bytes 12320 | tf_op jit(solution)/shard_map/all_to_all | solution.py:579
  34.3 0.6 %reshape.23 = f32[1,1,24,128]{3,2,1,0:T(8,128)} reshape(f32[8,3,128]{2,1,0:T(4,128)S(1)} %all-to-all-done) | data formatting | bytes 24576 | tf_op jit(solution)/shard_map/reshape | solution.py:595
Async XLA Ops:
  7.2 8.7 %collective-permute-start = (f32[1008,128]{1,0:T(8,128)S(1)}, f32[1008,128]{1,0:T(8,128)S(1)}, u32[]{:S(2)}, u32[]{:S(2)}) collective-permute-start(f32[1008,128]{1,0:T(8,128)S(1)} %get-tuple-element.27), channel_id=1, source_target_pairs={{0,1},{1,0},{2,3},{3,2},{4,5},{5,4},{6,7},{7,6},{8,9},{9,8},{10,11... | collective-permute-start | bytes 1548296 | tf_op jit(solution)/shard_map/ppermute | solution.py:480
  10.5 5.4 %collective-permute-start.2 = (f32[432,128]{1,0:T(8,128)S(1)}, f32[432,128]{1,0:T(8,128)S(1)}, u32[]{:S(2)}, u32[]{:S(2)}) collective-permute-start(f32[432,128]{1,0:T(8,128)S(1)} %get-tuple-element.31), channel_id=1, source_target_pairs={{0,255},{1,2},{2,1},{3,4},{4,3},{5,6},{6,5},{7,8},{8,7},{9,10},{10... | collective-permute-start | bytes 663560 | tf_op jit(solution)/shard_map/ppermute | solution.py:480
  10.5 19.2 %collective-permute-start.1 = (f32[576,128]{1,0:T(8,128)S(1)}, f32[576,128]{1,0:T(8,128)S(1)}, u32[]{:S(2)}, u32[]{:S(2)}) collective-permute-start(f32[576,128]{1,0:T(8,128)S(1)} %get-tuple-element.28), channel_id=1, source_target_pairs={{0,255},{1,2},{2,1},{3,4},{4,3},{5,6},{6,5},{7,8},{8,7},{9,10},{10... | collective-permute-start | bytes 884744 | tf_op jit(solution)/shard_map/ppermute | solution.py:480
  12.2 3.6 %copy-start = (s32[16,1]{0,1:T(1,128)S(1)}, s32[16,1]{0,1:T(1,128)}, u32[]{:S(2)}) copy-start(s32[16,1]{0,1:T(1,128)} %param.10) | copy-start | bytes 196
  15.4 4.0 %copy-start.1 = (f32[4608,128]{1,0:T(8,128)}, f32[4608,128]{1,0:T(8,128)S(1)}, u32[]{:S(2)}) copy-start(f32[4608,128]{1,0:T(8,128)S(1)} %get-tuple-element.25.acc_hbm) | copy-start | bytes 7077892
  19.3 15.0 %all-to-all-start = ((f32[8,3,128]{2,1,0:T(4,128)}), f32[8,3,128]{2,1,0:T(4,128)S(1)}, u32[]{:S(2)}, u32[]{:S(2)}) async-start(f32[8,3,128]{2,1,0:T(4,128)} %get-tuple-element.33), calls=%async_computation | async-start | bytes 32768 | tf_op jit(solution)/shard_map/all_to_all | solution.py:579
